TPU v7x, 256 devices: a whole 4x4x8 slice. The times are simulated.
256 devices in a mesh: ma: 64 (over z, y, core), ta: 4 (over x).
Axes of the slice: x: 4, y: 4, z: 8, core: 2. Of those that a mesh axis runs over, the one named last changes fastest.
Arguments:
- harmonics: float32 [4, 2, 64, 2, 8192], P('ta', None, 'ma'), may hold values from -0.01953125 to 0.01953125
- noise_weight: float32 [4, 64, 16384], P('ta', 'ma'), may hold values from 0.3 to 3
- order_table: int32 [64], replicated, may hold values from 0 to 8191, as said below
- curve_weight: float32 [2, 32], replicated, may hold values from -6 to 6
Outputs:
- kappa_map: float32 [4, 2, 64, 16384], P('ta', None, 'ma')
- euler_curve: float32 [2, 32], replicated
- alm_grad: float32 [4, 2, 64, 2, 8192], P('ta', None, 'ma')
Inputs may be any that keep to these rules, and one draw needn't show every extreme that they name: `order_table`: each interval of 128 orders that starts at a multiple of 128 holds exactly one entry; the 1 entries of each aligned run (the rows of one device) lie in 1 consecutive such intervals, in increasing order, the first of which has an index that is a multiple of 1.
All inputs are finite; a program needn't handle non-finite values.
Results may differ from a plain program's by a relative error of at most 0.0003.
Values sent between devices are 32-bit elements; how exact they have to be, the bound alone decides.
No kernel may reach another device: no remote copies, remote signals or barrier semaphores. Data moves between devices by JAX's collectives and lax.ppermute only.
A program may use at most 128 MiB of HBM per device.

v0:
```python
import math

import jax
import jax.numpy as jnp
from jax import lax
from jax.experimental import pallas as pl
from jax.experimental.pallas import tpu as pltpu
from jax.sharding import PartitionSpec as P

F32 = jnp.float32
HIGHEST = lax.Precision.HIGHEST
NPIX = 16384
LMAX = 8192
CYCLES = 64
LEVELS = 32
SIDE = 128
ROWS = 24
FAR = -1.0e9


def iota(shape, dim):
    return lax.broadcasted_iota(jnp.int32, shape, dim)


def dot(a, b, contract):
    return lax.dot_general(a, b, ((contract[:1], contract[1:]), ((), ())), precision=HIGHEST,
                           preferred_element_type=F32)


def slot_cycle(half, row):
    own = jnp.where(row < 16, row + 16 * half, -1)
    return jnp.where((row == 16) & (half == 0), 32, own)


def selector():
    shape = (CYCLES, 4 * ROWS)
    cycle, column = iota(shape, 0), iota(shape, 1)
    odd = (column >= 2 * ROWS).astype(jnp.int32)
    rest = column - 2 * ROWS * odd
    half = (rest >= ROWS).astype(jnp.int32)
    held = slot_cycle(half, rest - ROWS * half)
    mirrored = jnp.where(cycle > 32, 64 - cycle, cycle)
    sign = jnp.where((cycle > 32) & (odd == 1), -1.0, 1.0)
    return jnp.where(held == mirrored, sign, 0.0).astype(F32)


def turn_cos_sin(index, whole):
    quarter = whole // 4
    index = index & (whole - 1)
    quadrant = (index + quarter // 2) >> (quarter.bit_length() - 1)
    x = (index - quadrant * quarter).astype(F32) * (2.0 * math.pi / whole)
    y = x * x
    sine = x * (1.0 + y * (-1.0 / 6 + y * (1.0 / 120 + y * (-1.0 / 5040 + y * (1.0 / 362880)))))
    cosine = 1.0 + y * (-0.5 + y * (1.0 / 24 + y * (-1.0 / 720 + y * (1.0 / 40320 - y * (1.0 / 3628800)))))
    swap = (quadrant & 1) == 1
    c = jnp.where(swap, sine, cosine)
    s = jnp.where(swap, cosine, sine)
    c = jnp.where(((quadrant + 1) & 2) == 2, -c, c)
    s = jnp.where((quadrant & 2) == 2, -s, s)
    return c, s


def legendre_kernel(orders, harmonics, table, sent, first, second, coefficients):
    ma = lax.axis_index("ma")
    order = orders[ma]
    order_value = order.astype(F32)
    square = (SIDE, SIDE)
    lane, step = iota(square, 1), iota(square, 0)
    degree_index = (lane >> 1) * SIDE + step
    j = degree_index.astype(F32)
    degree = order_value + j
    alpha = jnp.sqrt(
        jnp.maximum((2.0 * degree - 1.0) * (2.0 * degree + 1.0), 0.0)
        / jnp.maximum(j * (j + 2.0 * order_value), 1.0)
    )
    beta = jnp.sqrt(
        jnp.maximum((j - 1.0) * (j - 1.0 + 2.0 * order_value), 0.0)
        / jnp.maximum((2.0 * degree - 3.0) * (2.0 * degree - 1.0), 1.0)
    )
    moving = degree_index > 0
    first[...] = jnp.where(moving, alpha, 0.0)
    second[...] = jnp.where(moving, -alpha * beta, 1.0)
    valid = degree_index < LMAX - order
    even_lane = (lane & 1) == 0
    for r in range(2):
        turned = harmonics[r].T
        real = jnp.where(even_lane, turned, pltpu.roll(turned, 1, 1))
        imag = jnp.where(even_lane, pltpu.roll(turned, SIDE - 1, 1), turned)
        coefficients[2 * r] = jnp.where(valid, real, 0.0)
        coefficients[2 * r + 1] = jnp.where(valid, imag, 0.0)

    shape = (ROWS, SIDE)
    row, half = iota(shape, 0), iota(shape, 1) & 1
    held = slot_cycle(half, row)
    z = jnp.where(held >= 0, 4.0 * (64.0 - 2.0 * held.astype(F32)) / (3.0 * NPIX), 0.0)
    below_one = 1.0 - (1.0 - z * z)
    log_term = -below_one * (1.0 + below_one * (0.5 + below_one * (1.0 / 3.0)))
    full = jnp.full(shape, order_value, F32)
    seed = jnp.exp(
        0.5 * jnp.log((2.0 * full + 1.0) / (4.0 * math.pi))
        - 0.25 * jnp.log(math.pi * (full + 0.25))
        + 0.5 * full * log_term
    )

    unroll = 8

    def compose(block, state):
        pu, pl_, qu, ql = state
        for s in range(unroll):
            i = block * unroll + s
            zc = z * first[pl.ds(i, 1), :]
            c2 = second[pl.ds(i, 1), :]
            pu, pl_ = zc * pu + c2 * pl_, pu
            qu, ql = zc * qu + c2 * ql, qu
        return pu, pl_, qu, ql

    ones, zeros = jnp.ones(shape, F32), jnp.zeros(shape, F32)
    a, c, b, d = lax.fori_loop(0, SIDE // unroll, compose, (ones, zeros, zeros, ones))
    lanes = iota(shape, 1)
    for by in (2, 4, 8, 16, 32, 64):
        inside = lanes >= by
        ea = jnp.where(inside, pltpu.roll(a, by, 1), 1.0)
        eb = jnp.where(inside, pltpu.roll(b, by, 1), 0.0)
        ec = jnp.where(inside, pltpu.roll(c, by, 1), 0.0)
        ed = jnp.where(inside, pltpu.roll(d, by, 1), 1.0)
        a, b, c, d = a * ea + b * ec, a * eb + b * ed, c * ea + d * ec, c * eb + d * ed
    started = lanes >= 2
    upper = jnp.where(started, pltpu.roll(b, 2, 1) * seed, 0.0)
    lower = jnp.where(started, pltpu.roll(d, 2, 1) * seed, seed)

    def advance(block, state):
        upper, lower, sums = state[0], state[1], list(state[2:])
        for s in range(unroll):
            i = block * unroll + s
            zc = z * first[pl.ds(i, 1), :]
            upper, lower = zc * upper + second[pl.ds(i, 1), :] * lower, upper
            table[i] = upper
            for f in range(4):
                at = 4 * (s % 2) + f
                sums[at] = sums[at] + coefficients[f, pl.ds(i, 1), :] * upper
        return (upper, lower, *sums)

    state = lax.fori_loop(0, SIDE // unroll, advance, (upper, lower) + (zeros,) * 8)
    sums = state[2:]
    pieces = []
    for parity in range(2):
        for which in range(2):
            total = None
            for f in range(4):
                pick = ((iota(square, 0) & 1) == which) & (iota(square, 1) == f)
                part = dot(sums[4 * parity + f], pick.astype(F32), (1, 0))
                total = part if total is None else total + part
            pieces.append(total)
    stacked = jnp.concatenate(pieces, axis=0)
    own = dot(selector(), stacked, (1, 0))
    before = pltpu.roll(own, 1, 0)
    after = pltpu.roll(own, CYCLES - 1, 0)
    sent[...] = own + pltpu.roll(before, 4, 1) + pltpu.roll(after, 8, 1)


def neighbour(x, by):
    lane = iota((SIDE, SIDE), 1)
    if by == 1:
        moved = pltpu.roll(x, SIDE - 1, 1)
        return jnp.where(lane == SIDE - 1, pltpu.roll(moved, SIDE - 1, 0), moved)
    moved = pltpu.roll(x, 1, 1)
    return jnp.where(lane == 0, pltpu.roll(moved, 1, 0), moved)


def euler_kernel(orders_row, level_weights, received, noise, noise_before, noise_after, kappa, sent,
                 fields, counts):
    cycle = lax.axis_index("ma")
    parity = (cycle + 1 + NPIX // 4 - CYCLES // 2) % 2
    square = (SIDE, SIDE)
    lane, row = iota(square, 1), iota(square, 0)
    order = jnp.concatenate([orders_row[...], orders_row[...]], axis=1)
    orders = jnp.broadcast_to(order, square)
    a_cos, a_sin = turn_cos_sin(orders * row, SIDE)
    orders_down = orders.astype(F32).T.astype(jnp.int32)
    b_cos, b_sin = turn_cos_sin(orders_down * lane, NPIX)
    basis = jnp.where(row < CYCLES, b_cos, b_sin)
    spin_cos, spin_sin = turn_cos_sin(jnp.broadcast_to(order, (8, SIDE)), 2 * NPIX)
    spin_cos, spin_sin = spin_cos[:1], spin_sin[:1]
    weight = jnp.where(order == 0, 1.0, 2.0)
    low = iota((1, SIDE), 1) < CYCLES

    flipped = jnp.concatenate([received[...], received[...]], axis=0).T
    lefts = []
    for kk in range(3):
        turned = parity == 1 if kk == 0 else parity == 0
        cs = jnp.where(turned, spin_cos, 1.0)
        sn = jnp.where(turned, spin_sin, 0.0)
        for r in range(2):
            real = flipped[4 * kk + 2 * r : 4 * kk + 2 * r + 1]
            imag = flipped[4 * kk + 2 * r + 1 : 4 * kk + 2 * r + 2]
            c_real = weight * (real * cs - imag * sn)
            c_imag = weight * (real * sn + imag * cs)
            u = jnp.where(low, c_real, -c_imag)
            v = jnp.where(low, -c_imag, -c_real)
            lefts.append(u * a_cos + v * a_sin)
    maps = dot(jnp.concatenate(lefts, axis=0), basis, (1, 0))

    def ratio(kk, r, weights):
        return 2.0 * (maps[(2 * kk + r) * SIDE : (2 * kk + r + 1) * SIDE] * weights)

    for r in range(2):
        kappa[r] = maps[r * SIDE : (r + 1) * SIDE]
        here = ratio(0, r, noise[...])
        above = jnp.where(cycle > 0, ratio(1, r, noise_before[...]), FAR)
        below = jnp.where(cycle < CYCLES - 1, ratio(2, r, noise_after[...]), FAR)
        odd = parity == 1
        fields[r, 0] = here
        fields[r, 1] = neighbour(here, 1)
        fields[r, 2] = neighbour(here, -1)
        fields[r, 3] = jnp.where(odd, below, neighbour(below, -1))
        fields[r, 4] = jnp.where(odd, neighbour(below, 1), below)
        fields[r, 5] = jnp.where(odd, above, neighbour(above, -1))
        fields[r, 6] = jnp.where(odd, neighbour(above, 1), above)

    counts[...] = jnp.zeros_like(counts)
    for r in range(2):

        def tile(index, carry, r=r):
            at = pl.ds(pl.multiple_of(index * 8, 8), 8)
            held = [fields[r, n, at, :] for n in range(7)]
            total = jnp.zeros((8, SIDE), F32)
            for t in range(LEVELS):
                twice = 2.0 * (-3.0 + 6.0 * t / (LEVELS - 1))
                u, e, w, d, dd, n1, n2 = [jnp.tanh(x - twice) for x in held]
                inner = e * (dd + n2) + w * (d + n1) + d * dd + n1 * n2 - 2.0
                total = total + (level_weights[r, t] * inner) * (1.0 - u * u)
                counts[r * LEVELS + t] += (1.0 + u) * (1.0 - dd) * (d + e)
            fields[r, 0, at, :] = total
            return carry

        lax.fori_loop(0, SIDE // 8, tile, 0)

    scale = 1.0 / (4.0 * math.sqrt(CYCLES * NPIX))
    duals = []
    for r in range(2):
        gradient = fields[r, 0] * (noise[...] * scale)
        sums = dot(gradient, basis, (1, 1))
        near = jnp.sum(sums * a_cos, axis=0, keepdims=True)
        far = jnp.sum(sums * a_sin, axis=0, keepdims=True)
        far = pltpu.roll(jnp.broadcast_to(far, (8, SIDE)), CYCLES, 1)[:1]
        both = near + jnp.where(low, -far, far)
        other = pltpu.roll(jnp.broadcast_to(both, (8, SIDE)), CYCLES, 1)[:1]
        cs = jnp.where(parity == 1, spin_cos, 1.0)
        sn = jnp.where(parity == 1, spin_sin, 0.0)
        duals.append(
            weight * jnp.where(low, both * cs - other * sn, -(both * cs + other * sn))
        )
    stacked = jnp.where(row == 0, duals[0], jnp.where(row == 1, duals[1], 0.0)).T
    per_order = stacked[:CYCLES] + pltpu.roll(stacked[CYCLES:], 2, 1)
    level_sums = jnp.sum(counts[...], axis=1) * -0.125
    padded = jnp.concatenate([jnp.zeros_like(level_sums), level_sums], axis=0)
    level_row = dot(jnp.ones((8, SIDE), F32), padded, (1, 1))[:1]
    sent[...] = per_order + level_row


def adjoint_kernel(orders, received, table, gradient, turned):
    order = orders[lax.axis_index("ma")]
    square = (SIDE, SIDE)
    lane, row = iota(square, 1), iota(square, 0)
    duals = dot(selector(), received[...], (0, 0))
    even = (iota((ROWS, SIDE), 1) & 1) == 0

    def column(parity, half, r, c):
        start = (2 * parity + half) * ROWS
        at = 2 * c + r
        return jnp.broadcast_to(duals[start : start + ROWS, at : at + 1], (ROWS, SIDE))

    factors = [
        [
            (
                jnp.where(even, column(parity, 0, r, 0), column(parity, 1, r, 1)),
                jnp.where(even, column(parity, 0, r, 1), column(parity, 1, r, 0)),
            )
            for r in range(2)
        ]
        for parity in range(2)
    ]

    def block(index, carry):
        rows = [[[], []], [[], []]]
        for s in range(8):
            values = table[index * 8 + s]
            for r in range(2):
                for kind in range(2):
                    product = values * factors[s % 2][r][kind]
                    rows[r][kind].append(jnp.sum(product, axis=0, keepdims=True))
        at = pl.ds(pl.multiple_of(index * 8, 8), 8)
        for r in range(2):
            straight = jnp.concatenate(rows[r][0], axis=0)
            crossed = jnp.concatenate(rows[r][1], axis=0)
            even_lane = (iota((8, SIDE), 1) & 1) == 0
            crossed = jnp.where(even_lane, pltpu.roll(crossed, SIDE - 1, 1), pltpu.roll(crossed, 1, 1))
            turned[r, at, :] = straight + crossed
        return carry

    lax.fori_loop(0, SIDE // 8, block, 0)
    for r in range(2):
        degree_index = (row >> 1) * SIDE + lane
        gradient[r] = jnp.where(degree_index < LMAX - order, turned[r].T, 0.0)


VMEM = pl.BlockSpec(memory_space=pltpu.VMEM)
SMEM = pl.BlockSpec(memory_space=pltpu.SMEM)
PARAMS = pltpu.CompilerParams(vmem_limit_bytes=40 * 1024 * 1024)


def shards(harmonics, noise_weight, order_table, curve_weight):
    ta_count = lax.axis_size("ta")
    ma_count = lax.axis_size("ma")
    noise = noise_weight.reshape(SIDE, SIDE)
    noise_before = lax.ppermute(noise, "ma", [(i, i + 1) for i in range(ma_count - 1)])
    noise_after = lax.ppermute(noise, "ma", [(i + 1, i) for i in range(ma_count - 1)])
    packed = harmonics.reshape(2, 2, 64, SIDE).transpose(0, 2, 1, 3).reshape(2, SIDE, SIDE)
    square = jax.ShapeDtypeStruct((CYCLES, SIDE), F32)
    table, sent = pl.pallas_call(
        legendre_kernel,
        in_specs=[SMEM, VMEM],
        out_specs=[VMEM, VMEM],
        out_shape=[jax.ShapeDtypeStruct((SIDE, ROWS, SIDE), F32), square],
        scratch_shapes=[
            pltpu.VMEM((SIDE, SIDE), F32),
            pltpu.VMEM((SIDE, SIDE), F32),
            pltpu.VMEM((4, SIDE, SIDE), F32),
        ],
        compiler_params=PARAMS,
        name="legendre",
    )(order_table, packed)
    received = lax.all_to_all(sent, "ma", split_axis=0, concat_axis=0, tiled=True)
    kappa, sent = pl.pallas_call(
        euler_kernel,
        in_specs=[VMEM, SMEM, VMEM, VMEM, VMEM, VMEM],
        out_specs=[VMEM, VMEM],
        out_shape=[jax.ShapeDtypeStruct((2, SIDE, SIDE), F32), square],
        scratch_shapes=[
            pltpu.VMEM((2, 7, SIDE, SIDE), F32),
            pltpu.VMEM((2 * LEVELS, 8, SIDE), F32),
        ],
        compiler_params=PARAMS,
        name="euler",
    )(order_table.reshape(1, CYCLES), curve_weight, received, noise, noise_before, noise_after)
    received = lax.all_to_all(sent, "ma", split_axis=0, concat_axis=0, tiled=True)
    counts = jnp.sum(received[:, CYCLES:], axis=0).reshape(2, LEVELS)
    one, two, three = [lax.ppermute(counts, "ta", [(i, i ^ by) for i in range(ta_count)]) for by in (1, 2, 3)]
    curve = ((counts + one) + (two + three)) / (ta_count * CYCLES * NPIX)
    gradient = pl.pallas_call(
        adjoint_kernel,
        in_specs=[SMEM, VMEM, VMEM],
        out_specs=VMEM,
        out_shape=jax.ShapeDtypeStruct((2, SIDE, SIDE), F32),
        scratch_shapes=[pltpu.VMEM((2, SIDE, SIDE), F32)],
        compiler_params=PARAMS,
        name="adjoint",
    )(order_table, received, table)
    gradient = gradient.reshape(2, 64, 2, SIDE).transpose(0, 2, 1, 3).reshape(1, 2, 1, 2, LMAX)
    return kappa.reshape(1, 2, 1, NPIX), curve, gradient


def solution(mesh):
    in_specs = (P("ta", None, "ma", None, None), P("ta", "ma", None), P(), P())
    out_specs = (P("ta", None, "ma", None), P(), P("ta", None, "ma", None, None))
    return jax.shard_map(shards, mesh=mesh, in_specs=in_specs, out_specs=out_specs, check_vma=False)
```

profile of v0, /device:TPU:1, one launch (start us, length us, event | category | flops | bytes accessed | tf_op | source)
XLA Modules:
  0.0 66.5 jit_solution(5822658549596495525)
XLA Ops:
  0.6 5.2 %collective-permute-start.1 = (f32[128,128]{1,0:T(8,128)}, f32[128,128]{1,0:T(8,128)S(1)}, u32[]{:S(2)}, u32[]{:S(2)}) collective-permute-start(f32[128,128]{1,0:T(8,128)} %bitcast.25), channel_id=1, source_target_pairs={{4,0},{8,4},{12,8},{16,12},{20,16},{24,20},{28,24},{32,28},{36,32}... | collective-permute-start | bytes 196616 | tf_op jit(solution)/shard_map/ppermute | solution.py:317
  5.8 1.9 %collective-permute-start = (f32[128,128]{1,0:T(8,128)}, f32[128,128]{1,0:T(8,128)S(1)}, u32[]{:S(2)}, u32[]{:S(2)}) collective-permute-start(f32[128,128]{1,0:T(8,128)} %bitcast.26), channel_id=1, source_target_pairs={{0,4},{4,8},{8,12},{12,16},{16,20},{20,24},{24,28},{28,32},{32,36}... | collective-permute-start | bytes 196616 | tf_op jit(solution)/shard_map/ppermute | solution.py:316
  7.7 0.0 copy-start
  7.7 0.9 %copy-done = f32[1,2,1,2,8192]{4,3,2,1,0:T(2,128)S(1)} copy-done((f32[1,2,1,2,8192]{4,3,2,1,0:T(2,128)S(1)}, f32[1,2,1,2,8192]{4,3,2,1,0:T(2,128)}, u32[]{:S(2)}) %copy-start) | copy-done | bytes 131096
  8.6 0.7 copy-done.2
  9.3 3.8 %legendre.1 = (f32[128,24,128]{2,1,0:T(8,128)S(1)}, f32[64,128]{1,0:T(8,128)S(1)}) custom-call(s32[64]{0:T(128)S(1)} %copy-done.2, f32[2,128,128]{2,1,0:T(8,128)S(1)} %bitcast.24), custom_call_target="tpu_custom_call" | custom-call | tf_op jit(solution)/shard_map/legendre/pallas_call | solution.py:320
  13.1 22.2 %all_to_all.22 = f32[64,1,128]{2,1,0:T(1,128)S(1)} all-to-all(f32[64,1,128]{2,1,0:T(1,128)S(1)} %bitcast.29), channel_id=1, replica_groups=mesh['ma'=64,'ta'=4] {'ma'}, dimensions={0} | all-to-all | bytes 65536 | tf_op jit(solution)/shard_map/all_to_all | solution.py:333
  35.3 0.0 collective-permute-done.1.noise_after
  35.3 0.0 collective-permute-done.noise_before
  35.3 0.8 %copy-done.1 = f32[1,1,16384]{2,1,0:T(1,128)S(1)} copy-done((f32[1,1,16384]{2,1,0:T(1,128)S(1)}, f32[1,1,16384]{2,1,0:T(1,128)}, u32[]{:S(2)}) %copy-start.1) | copy-done | bytes 65560
  36.1 0.7 %copy-done.4 = f32[2,32]{1,0:T(2,128)S(1)} copy-done((f32[2,32]{1,0:T(2,128)S(1)}, f32[2,32]{1,0:T(2,128)}, u32[]{:S(2)}) %copy-start.4) | copy-done | bytes 280
  36.8 8.3 %euler.1 = (f32[2,128,128]{2,1,0:T(8,128)}, f32[64,128]{1,0:T(8,128)S(1)}) custom-call(s32[1,64]{1,0:T(1,128)S(1)} %bitcast.30, f32[2,32]{1,0:T(2,128)S(1)} %copy-done.4, f32[64,128]{1,0:T(8,128)S(1)} %bitcast.23, f32[128,128]{1,0:T(8,128)S(1)} %bitcast.27, f32[128,128]{1,0:T(8,128)S(1)} %collective-permute-done.noise_before, ...), custom_call_target="tpu_custom_call" | custom-call | tf_op jit(solution)/shard_map/euler/pallas_call | solution.py:334
  45.1 13.4 %all_to_all.23 = f32[64,1,128]{2,1,0:T(1,128)S(1)} all-to-all(f32[64,1,128]{2,1,0:T(1,128)S(1)} %bitcast.28), channel_id=1, replica_groups=mesh['ma'=64,'ta'=4] {'ma'}, dimensions={0} | all-to-all | bytes 65536 | tf_op jit(solution)/shard_map/all_to_all | solution.py:346
  58.4 0.1 slice_reduce_fusion
  58.5 0.1 reshape.39
  58.6 2.5 %collective-permute-start.4 = (f32[2,32]{1,0:T(2,128)S(1)}, f32[2,32]{1,0:T(2,128)S(1)}, u32[]{:S(2)}, u32[]{:S(2)}) collective-permute-start(f32[2,32]{1,0:T(2,128)S(1)} %reshape.39), channel_id=1, source_target_pairs={{0,3},{1,2},{2,1},{3,0},{4,7},{5,6},{6,5},{7,4},{8,11},{9,10},{10,... | collective-permute-start | bytes 776 | tf_op jit(solution)/shard_map/ppermute | solution.py:348
  61.1 0.5 collective-permute-start.3
  61.6 0.3 collective-permute-start.2
  61.9 0.7 copy-done.3
  62.5 3.4 %adjoint.1 = f32[2,128,128]{2,1,0:T(8,128)} custom-call(s32[64]{0:T(128)S(1)} %copy-done.3, f32[64,128]{1,0:T(8,128)S(1)} %bitcast.22, f32[128,24,128]{2,1,0:T(8,128)S(1)} %get-tuple-element.10.table), custom_call_target="tpu_custom_call" | custom-call | tf_op jit(solution)/shard_map/adjoint/pallas_call | solution.py:350
  65.9 0.0 collective-permute-done.4
  65.9 0.0 collective-permute-done.3
  65.9 0.0 collective-permute-done.2
  65.9 0.6 add_multiply_fusion
  (4 shorter events, 0.0 us)
Async XLA Ops:
  0.6 34.6 %collective-permute-start.1 = (f32[128,128]{1,0:T(8,128)}, f32[128,128]{1,0:T(8,128)S(1)}, u32[]{:S(2)}, u32[]{:S(2)}) collective-permute-start(f32[128,128]{1,0:T(8,128)} %bitcast.25), channel_id=1, source_target_pairs={{4,0},{8,4},{12,8},{16,12},{20,16},{24,20},{28,24},{32,28},{36,32}... | collective-permute-start | bytes 196616 | tf_op jit(solution)/shard_map/ppermute | solution.py:317
  5.8 29.5 %collective-permute-start = (f32[128,128]{1,0:T(8,128)}, f32[128,128]{1,0:T(8,128)S(1)}, u32[]{:S(2)}, u32[]{:S(2)}) collective-permute-start(f32[128,128]{1,0:T(8,128)} %bitcast.26), channel_id=1, source_target_pairs={{0,4},{4,8},{8,12},{12,16},{16,20},{20,24},{24,28},{28,32},{32,36}... | collective-permute-start | bytes 196616 | tf_op jit(solution)/shard_map/ppermute | solution.py:316
  7.7 0.9 %copy-start = (f32[1,2,1,2,8192]{4,3,2,1,0:T(2,128)S(1)}, f32[1,2,1,2,8192]{4,3,2,1,0:T(2,128)}, u32[]{:S(2)}) copy-start(f32[1,2,1,2,8192]{4,3,2,1,0:T(2,128)} %param.4) | copy-start | bytes 393220
  8.6 0.7 copy-start.2
  35.3 0.8 %copy-start.1 = (f32[1,1,16384]{2,1,0:T(1,128)S(1)}, f32[1,1,16384]{2,1,0:T(1,128)}, u32[]{:S(2)}) copy-start(f32[1,1,16384]{2,1,0:T(1,128)} %param.5) | copy-start | bytes 196612
  36.1 0.7 %copy-start.4 = (f32[2,32]{1,0:T(2,128)S(1)}, f32[2,32]{1,0:T(2,128)}, u32[]{:S(2)}) copy-start(f32[2,32]{1,0:T(2,128)} %level_weights.1) | copy-start | bytes 772
  58.6 7.3 %collective-permute-start.4 = (f32[2,32]{1,0:T(2,128)S(1)}, f32[2,32]{1,0:T(2,128)S(1)}, u32[]{:S(2)}, u32[]{:S(2)}) collective-permute-start(f32[2,32]{1,0:T(2,128)S(1)} %reshape.39), channel_id=1, source_target_pairs={{0,3},{1,2},{2,1},{3,0},{4,7},{5,6},{6,5},{7,4},{8,11},{9,10},{10,... | collective-permute-start | bytes 776 | tf_op jit(solution)/shard_map/ppermute | solution.py:348
  61.1 4.8 %collective-permute-start.3 = (f32[2,32]{1,0:T(2,128)S(1)}, f32[2,32]{1,0:T(2,128)S(1)}, u32[]{:S(2)}, u32[]{:S(2)}) collective-permute-start(f32[2,32]{1,0:T(2,128)S(1)} %reshape.39), channel_id=1, source_target_pairs={{0,2},{1,3},{2,0},{3,1},{4,6},{5,7},{6,4},{7,5},{8,10},{9,11},{10,... | collective-permute-start | bytes 776 | tf_op jit(solution)/shard_map/ppermute | solution.py:348
  61.6 4.3 %collective-permute-start.2 = (f32[2,32]{1,0:T(2,128)S(1)}, f32[2,32]{1,0:T(2,128)S(1)}, u32[]{:S(2)}, u32[]{:S(2)}) collective-permute-start(f32[2,32]{1,0:T(2,128)S(1)} %reshape.39), channel_id=1, source_target_pairs={{0,1},{1,0},{2,3},{3,2},{4,5},{5,4},{6,7},{7,6},{8,9},{9,8},{10,11... | collective-permute-start | bytes 776 | tf_op jit(solution)/shard_map/ppermute | solution.py:348
  61.9 0.7 copy-start.3
where the time goes:
time: 66.8 us; the launch traced here: 66.5 us
  blocking collectives  35.6 us (53%)
  Pallas kernels  15.4 us (23%)
  starting transfers between devices  10.3 us (15%)
  local copies, waits for them, and re-layouts  3.81 us (6%)
  between operations  0.68 us (1%)
    all_to_all x2, blocking collectives, shards(): lax.all_to_all(sent, 'ma', split_axis=0, concat_axis=0, tiled=True)  35.6 us
    pallas_call x1, Pallas kernels, shards(): pl.pallas_call(euler_kernel, in_specs=[VMEM, SMEM, VMEM, VMEM, VMEM, VMEM...  8.28 us
    ppermute x1, starting transfers between devices, shards(): lax.ppermute(noise, 'ma', [(i + 1, i) for i in range(ma_count - 1)])  5.15 us
    pallas_call x1, Pallas kernels, shards(): pl.pallas_call(legendre_kernel, in_specs=[SMEM, VMEM], out_specs=[VMEM, V...  3.77 us
    unnamed x10, local copies, waits for them, and re-layouts  3.72 us
    pallas_call x1, Pallas kernels, shards(): pl.pallas_call(adjoint_kernel, in_specs=[SMEM, VMEM, VMEM], out_specs=VME...  3.36 us
    ppermute x3, starting transfers between devices, shards(): lax.ppermute(counts, 'ta', [(i, i ^ by) for i in range(ta_count)])  3.26 us
    ppermute x1, starting transfers between devices, shards(): lax.ppermute(noise, 'ma', [(i, i + 1) for i in range(ma_count - 1)])  1.92 us
  transfers between devices with their start and end apart: 5, of which 0 were waited for; matrix products, arithmetic and copies ran while one was open for 0% of the time, Pallas kernels for 11%

commit v1 on v0

v1 whole, which is shorter than its diff:
```python
import math

import jax
import jax.numpy as jnp
from jax import lax
from jax.experimental import pallas as pl
from jax.experimental.pallas import tpu as pltpu
from jax.sharding import PartitionSpec as P

F32 = jnp.float32
BF16 = jnp.bfloat16
HIGHEST = lax.Precision.HIGHEST
NPIX = 16384
LMAX = 8192
CYCLES = 64
LEVELS = 32
SIDE = 128
ROWS = 24
TILE = 16
FAR = -1.0e9


def iota(shape, dim):
    return lax.broadcasted_iota(jnp.int32, shape, dim)


def dot(a, b, contract):
    return lax.dot_general(a, b, ((contract[:1], contract[1:]), ((), ())), precision=HIGHEST,
                           preferred_element_type=F32)


def slot_cycle(half, row):
    own = jnp.where(row < 16, row + 16 * half, -1)
    return jnp.where((row == 16) & (half == 0), 32, own)


def selection(cycle, odd, half, row):
    mirrored = jnp.where(cycle > 32, 64 - cycle, cycle)
    sign = jnp.where((cycle > 32) & odd, -1.0, 1.0)
    return jnp.where(slot_cycle(half, row) == mirrored, sign, 0.0).astype(F32)


def split(x):
    high = x.astype(BF16)
    return high, (x - high.astype(F32)).astype(BF16)


def mxu(a, b):
    return lax.dot_general(a, b, (((1,), (0,)), ((), ())), preferred_element_type=F32)


def turn_cos_sin(index, whole):
    quarter = whole // 4
    index = index & (whole - 1)
    quadrant = (index + quarter // 2) >> (quarter.bit_length() - 1)
    x = (index - quadrant * quarter).astype(F32) * (2.0 * math.pi / whole)
    y = x * x
    sine = x * (1.0 + y * (-1.0 / 6 + y * (1.0 / 120 + y * (-1.0 / 5040 + y * (1.0 / 362880)))))
    cosine = 1.0 + y * (-0.5 + y * (1.0 / 24 + y * (-1.0 / 720 + y * (1.0 / 40320 - y * (1.0 / 3628800)))))
    swap = (quadrant & 1) == 1
    c = jnp.where(swap, sine, cosine)
    s = jnp.where(swap, cosine, sine)
    c = jnp.where(((quadrant + 1) & 2) == 2, -c, c)
    s = jnp.where((quadrant & 2) == 2, -s, s)
    return c, s


def make_basis(orders_row, turns, basis, basis_turned, small):
    square = (SIDE, SIDE)
    lane, row = iota(square, 1), iota(square, 0)
    twice = (iota((CYCLES, SIDE), 1) >> 1) == iota((CYCLES, SIDE), 0)
    eight = jnp.broadcast_to(orders_row[...].astype(F32), (8, CYCLES))
    eight = dot(eight, twice.astype(F32), (1, 0)).astype(jnp.int32)
    orders = jnp.broadcast_to(eight[:1], square)
    turns[0], turns[1] = turn_cos_sin(orders * row, SIDE)
    cosine, sine = turn_cos_sin(orders * row, NPIX)
    turned = jnp.where((lane & 1) == 0, cosine, sine)
    for ref, value in ((basis, turned.T), (basis_turned, turned)):
        ref[:, :SIDE], ref[:, SIDE:] = split(value)
    small[0], small[1] = turn_cos_sin(eight, 2 * NPIX)
    small[2] = jnp.where(eight == 0, 1.0, 2.0)


def legendre_kernel(orders_in, row_in, harmonics_in, table, sent, order_out, turns, basis, basis_turned, small_out,
                    first, second, coefficients, orders, harmonics, orders_row, sems):
    ma = lax.axis_index("ma")
    fetch_orders = pltpu.make_async_copy(orders_in, orders, sems.at[0])
    fetch_harmonics = pltpu.make_async_copy(harmonics_in, harmonics, sems.at[1])
    fetch_row = pltpu.make_async_copy(row_in, orders_row, sems.at[2])
    fetch_orders.start()
    fetch_row.start()
    fetch_harmonics.start()
    fetch_orders.wait()
    order = orders[ma]
    order_out[...] = jnp.full(order_out.shape, order, jnp.int32)
    order_value = order.astype(F32)
    square = (SIDE, SIDE)
    lane, step = iota(square, 1), iota(square, 0)
    degree_index = (lane >> 1) * SIDE + step
    j = degree_index.astype(F32)
    degree = order_value + j
    alpha = jnp.sqrt(
        jnp.maximum((2.0 * degree - 1.0) * (2.0 * degree + 1.0), 0.0)
        / jnp.maximum(j * (j + 2.0 * order_value), 1.0)
    )
    beta = jnp.sqrt(
        jnp.maximum((j - 1.0) * (j - 1.0 + 2.0 * order_value), 0.0)
        / jnp.maximum((2.0 * degree - 3.0) * (2.0 * degree - 1.0), 1.0)
    )
    moving = degree_index > 0
    first[...] = jnp.where(moving, alpha, 0.0)
    second[...] = jnp.where(moving, -alpha * beta, 1.0)
    shape = (ROWS, SIDE)
    row, half = iota(shape, 0), iota(shape, 1) & 1
    held = slot_cycle(half, row)
    z = jnp.where(held >= 0, 4.0 * (64.0 - 2.0 * held.astype(F32)) / (3.0 * NPIX), 0.0)
    below_one = 1.0 - (1.0 - z * z)
    log_term = -below_one * (1.0 + below_one * (0.5 + below_one * (1.0 / 3.0)))
    full = jnp.full(shape, order_value, F32)
    seed = jnp.exp(
        0.5 * jnp.log((2.0 * full + 1.0) / (4.0 * math.pi))
        - 0.25 * jnp.log(math.pi * (full + 0.25))
        + 0.5 * full * log_term
    )

    unroll = 8

    def compose(block, state):
        pu, pl_, qu, ql = state
        for s in range(unroll):
            i = block * unroll + s
            zc = z * first[pl.ds(i, 1), :]
            c2 = second[pl.ds(i, 1), :]
            pu, pl_ = zc * pu + c2 * pl_, pu
            qu, ql = zc * qu + c2 * ql, qu
        return pu, pl_, qu, ql

    fetch_row.wait()
    make_basis(orders_row, turns, basis, basis_turned, small_out)
    ones, zeros = jnp.ones(shape, F32), jnp.zeros(shape, F32)
    a, c, b, d = lax.fori_loop(0, SIDE // unroll, compose, (ones, zeros, zeros, ones))
    lanes = iota(shape, 1)
    for by in (2, 4, 8, 16, 32, 64):
        inside = lanes >= by
        ea = jnp.where(inside, pltpu.roll(a, by, 1), 1.0)
        eb = jnp.where(inside, pltpu.roll(b, by, 1), 0.0)
        ec = jnp.where(inside, pltpu.roll(c, by, 1), 0.0)
        ed = jnp.where(inside, pltpu.roll(d, by, 1), 1.0)
        a, b, c, d = a * ea + b * ec, a * eb + b * ed, c * ea + d * ec, c * eb + d * ed
    started = lanes >= 2
    upper = jnp.where(started, pltpu.roll(b, 2, 1) * seed, 0.0)
    lower = jnp.where(started, pltpu.roll(d, 2, 1) * seed, seed)

    fetch_harmonics.wait()
    valid = degree_index < LMAX - order
    even_lane = (lane & 1) == 0
    for r in range(2):
        turned = harmonics[r].T
        real = jnp.where(even_lane, turned, pltpu.roll(turned, 1, 1))
        imag = jnp.where(even_lane, pltpu.roll(turned, SIDE - 1, 1), turned)
        coefficients[2 * r] = jnp.where(valid, real, 0.0)
        coefficients[2 * r + 1] = jnp.where(valid, imag, 0.0)

    def advance(block, state):
        upper, lower, sums = state[0], state[1], list(state[2:])
        for s in range(unroll):
            i = block * unroll + s
            zc = z * first[pl.ds(i, 1), :]
            upper, lower = zc * upper + second[pl.ds(i, 1), :] * lower, upper
            table[i] = upper
            for f in range(4):
                at = 4 * (s % 2) + f
                sums[at] = sums[at] + coefficients[f, pl.ds(i, 1), :] * upper
        return (upper, lower, *sums)

    state = lax.fori_loop(0, SIDE // unroll, advance, (upper, lower) + (zeros,) * 8)
    sums = state[2:]
    high, low = split(jnp.concatenate(sums, axis=0))
    alike = ((iota(square, 0) & 1) == (iota(square, 1) & 1)).astype(BF16)
    sums = mxu(jnp.concatenate([high, low], axis=1), jnp.concatenate([alike, alike], axis=0))
    small = (2 * ROWS, SIDE)
    pair, lane_half = iota(small, 1) >> 1, iota(small, 1) & 1
    held_sums = jnp.zeros(small, F32)
    for f in range(4):
        both = [sums[(4 * parity + f) * ROWS : (4 * parity + f + 1) * ROWS] for parity in range(2)]
        held_sums = jnp.where(pair == f, jnp.concatenate(both, axis=0), held_sums)
    halves = jnp.concatenate([jnp.where(lane_half == half, held_sums, 0.0) for half in range(2)], axis=0)
    high, low = split(halves)
    sel = (2 * CYCLES, 4 * ROWS)
    at_row = iota(sel, 1)
    in_half = (at_row >= 2 * ROWS).astype(jnp.int32)
    at_row = at_row - 2 * ROWS * in_half
    odd = (at_row >= ROWS).astype(jnp.int32)
    pick = selection(iota(sel, 0) >> 1, odd == 1, in_half, at_row - ROWS * odd).astype(BF16)
    own = mxu(jnp.concatenate([pick, pick], axis=1), jnp.concatenate([high, low], axis=0))
    even_lane = (iota(square, 1) & 1) == 0
    own = own + jnp.where(even_lane, pltpu.roll(own, SIDE - 1, 1), pltpu.roll(own, 1, 1))
    own = jnp.where(iota(square, 1) < 8, own, 0.0)
    before = pltpu.roll(own, 2, 0)
    after = pltpu.roll(own, 2 * CYCLES - 2, 0)
    sent[...] = own + pltpu.roll(before, 8, 1) + pltpu.roll(after, 16, 1)


def both_halves(a, pair):
    product = mxu(jnp.concatenate(split(a), axis=1), jnp.concatenate([pair, pair], axis=0))
    return product[:, :SIDE] + product[:, SIDE:]


def swapped(x):
    x = jnp.broadcast_to(x, (8, SIDE))
    even = (iota((8, SIDE), 1) & 1) == 0
    return jnp.where(even, pltpu.roll(x, SIDE - 1, 1), pltpu.roll(x, 1, 1))[:1]


def neighbour(x, by):
    lane = iota((SIDE, SIDE), 1)
    if by == 1:
        moved = pltpu.roll(x, SIDE - 1, 1)
        return jnp.where(lane == SIDE - 1, pltpu.roll(moved, SIDE - 1, 0), moved)
    moved = pltpu.roll(x, 1, 1)
    return jnp.where(lane == 0, pltpu.roll(moved, 1, 0), moved)


def euler_kernel(weights_in, turns, basis, basis_turned, small, received, noise_in, within, across, kappa_out, sent,
                 fields, counts, level_weights, noise, kappa, sems):
    fetch_weights = pltpu.make_async_copy(weights_in, level_weights, sems.at[0])
    fetch_noise = pltpu.make_async_copy(noise_in, noise, sems.at[1])
    fetch_weights.start()
    fetch_noise.start()
    cycle = lax.axis_index("ma")
    parity = (cycle + 1 + NPIX // 4 - CYCLES // 2) % 2
    square = (SIDE, SIDE)
    row = iota(square, 0)
    a_cos, a_sin = turns[0], turns[1]
    spin_cos, spin_sin, weight = small[0, :1], small[1, :1], small[2, :1]
    low = (iota((1, SIDE), 1) & 1) == 0

    flipped = received[...].T
    lefts = []
    for kk in range(3):
        turned = parity == 1 if kk == 0 else parity == 0
        cs = jnp.where(turned, spin_cos, 1.0)
        sn = jnp.where(turned, spin_sin, 0.0)
        for r in range(2):
            real = flipped[8 * kk + 4 * r : 8 * kk + 4 * r + 1]
            imag = flipped[8 * kk + 4 * r + 2 : 8 * kk + 4 * r + 3]
            c_real = weight * (real * cs - imag * sn)
            c_imag = weight * (real * sn + imag * cs)
            u = jnp.where(low, c_real, -c_imag)
            v = jnp.where(low, -c_imag, -c_real)
            lefts.append(u * a_cos + v * a_sin)
    maps = both_halves(jnp.concatenate(lefts, axis=0), basis[...])

    for r in range(2):
        kappa[r] = maps[r * SIDE : (r + 1) * SIDE]
    keep_kappa = pltpu.make_async_copy(kappa, kappa_out, sems.at[2])
    keep_kappa.start()
    fetch_noise.wait()

    second_of_chip = cycle % 2 == 1
    noise_before = jnp.where(second_of_chip, within[...], across[...])
    noise_after = jnp.where(second_of_chip, across[...], within[...])

    def ratio(kk, r, weights):
        return 2.0 * (maps[(2 * kk + r) * SIDE : (2 * kk + r + 1) * SIDE] * weights)

    odd = parity == 1

    def aside(x):
        by = jnp.where(odd, SIDE - 1, 1)
        moved = pltpu.roll(x, by, 1)
        edge = jnp.where(odd, SIDE - 1, 0)
        return jnp.where(iota(square, 1) == edge, pltpu.roll(moved, by, 0), moved)

    for r in range(2):
        here = ratio(0, r, noise[...])
        above = jnp.where(cycle > 0, ratio(1, r, noise_before), FAR)
        below = jnp.where(cycle < CYCLES - 1, ratio(2, r, noise_after), FAR)
        fields[r, 0] = here
        fields[r, 1] = neighbour(here, 1)
        fields[r, 2] = neighbour(here, -1)
        moved_below, moved_above = aside(below), aside(above)
        fields[r, 3] = jnp.where(odd, below, moved_below)
        fields[r, 4] = jnp.where(odd, moved_below, below)
        fields[r, 5] = jnp.where(odd, above, moved_above)
        fields[r, 6] = jnp.where(odd, moved_above, above)

    counts[...] = jnp.zeros_like(counts)
    fetch_weights.wait()
    def sweep(top):
        for r in range(2):

            def tile(index, carry, r=r):
                at = pl.ds(pl.multiple_of(index * TILE, TILE), TILE)
                held = [fields[r, n, at, :] for n in range(5 if top else 7)]
                total = jnp.zeros((TILE, SIDE), F32)
                for t in range(LEVELS):
                    twice = 2.0 * (-3.0 + 6.0 * t / (LEVELS - 1))
                    u, e, w, d, dd, *others = [jnp.tanh(x - twice) for x in held]
                    n1, n2 = others if others else (-1.0, -1.0)
                    down = dd * (d + e)
                    up = 1.0 - e if top else n2 * (e + n1)
                    inner = down + up + w * (d + n1) - 2.0
                    scaled = level_weights[r, t] * u
                    total = total + inner * (level_weights[r, t] - scaled * u)
                    part = u * (2.0 - down - up) if top else u * (2.0 - down)
                    counts[r * LEVELS + t] += jnp.sum(part.reshape(TILE // 8, 8, SIDE), axis=0)
                fields[r, 0, at, :] = total
                return carry

            lax.fori_loop(0, SIDE // TILE, tile, 0)

    pl.when(cycle == 0)(lambda: sweep(True))
    pl.when(cycle > 0)(lambda: sweep(False))

    scale = 1.0 / (4.0 * math.sqrt(CYCLES * NPIX))
    duals = []
    gradients = jnp.concatenate([fields[r, 0] * (noise[...] * scale) for r in range(2)], axis=0)
    all_sums = both_halves(gradients, basis_turned[...])
    for r in range(2):
        sums = all_sums[r * SIDE : (r + 1) * SIDE]
        near = jnp.sum(sums * a_cos, axis=0, keepdims=True)
        far = jnp.sum(sums * a_sin, axis=0, keepdims=True)
        far = swapped(far)
        both = near + jnp.where(low, -far, far)
        other = swapped(both)
        cs = jnp.where(parity == 1, spin_cos, 1.0)
        sn = jnp.where(parity == 1, spin_sin, 0.0)
        duals.append(
            weight * jnp.where(low, both * cs - other * sn, -(both * cs + other * sn))
        )
    stacked = jnp.where(row == 0, duals[0], jnp.where(row == 1, duals[1], 0.0)).T
    level_sums = jnp.sum(counts[...], axis=1) * -0.125
    level_sums = level_sums + jnp.where(cycle == 0, 2.0 * NPIX / 8.0 / SIDE, 0.0)
    padded = jnp.concatenate([jnp.zeros_like(level_sums), level_sums], axis=0)
    level_row = dot(jnp.ones((8, SIDE), F32), padded, (1, 1))[:1]
    sent[...] = stacked + level_row
    keep_kappa.wait()


def adjoint_kernel(order_rows, received, table, gradient, turned):
    order = order_rows[:1]
    square = (SIDE, SIDE)
    lane, row = iota(square, 1), iota(square, 0)
    arrived = jnp.where(lane < CYCLES, received[...], 0.0)
    real = (row & 1) == 0
    pairs = jnp.where(real, arrived, 0.0) + pltpu.roll(jnp.where(real, 0.0, arrived), 2, 1)
    sel = (4 * ROWS, SIDE)
    at_row = iota(sel, 0)
    odd = (at_row >= 2 * ROWS).astype(jnp.int32)
    at_row = at_row - 2 * ROWS * odd
    in_half = (at_row >= ROWS).astype(jnp.int32)
    pick = selection(iota(sel, 1) >> 1, odd == 1, in_half, at_row - ROWS * in_half).astype(BF16)
    duals = mxu(jnp.concatenate([pick, pick], axis=1), jnp.concatenate(split(pairs), axis=0))
    even = (iota((ROWS, SIDE), 1) & 1) == 0

    def column(parity, half, r, c):
        start = (2 * parity + half) * ROWS
        at = 2 * c + r
        return jnp.broadcast_to(duals[start : start + ROWS, at : at + 1], (ROWS, SIDE))

    factors = [
        [
            (
                jnp.where(even, column(parity, 0, r, 0), column(parity, 1, r, 1)),
                jnp.where(even, column(parity, 0, r, 1), column(parity, 1, r, 0)),
            )
            for r in range(2)
        ]
        for parity in range(2)
    ]

    sub = iota((8, SIDE), 0)

    def merge(a, b, by):
        mine = (sub & by) == 0
        return jnp.where(mine, a, b) + pltpu.roll(jnp.where(mine, b, a), 8 - by, 0)

    even_lane = (iota((8, SIDE), 1) & 1) == 0

    def block(index, carry):
        at = pl.ds(pl.multiple_of(index * 8, 8), 8)
        values = [table[index * 8 + s] for s in range(8)]
        for r in range(2):
            summed = []
            for kind in range(2):
                parts = []
                for s in range(8):
                    product = values[s] * factors[s % 2][r][kind]
                    parts.append(product[:8] + product[8:16] + product[16:])
                for by in (1, 2, 4):
                    parts = [merge(a, b, by) for a, b in zip(parts[::2], parts[1::2])]
                summed.append(parts[0])
            straight, crossed = summed
            crossed = jnp.where(even_lane, pltpu.roll(crossed, SIDE - 1, 1), pltpu.roll(crossed, 1, 1))
            turned[r, at, :] = straight + crossed
        return carry

    lax.fori_loop(0, SIDE // 8, block, 0)
    for r in range(2):
        degree_index = (row >> 1) * SIDE + lane
        gradient[r] = jnp.where(degree_index < LMAX - order, turned[r].T, 0.0)


VMEM = pl.BlockSpec(memory_space=pltpu.VMEM)
SMEM = pl.BlockSpec(memory_space=pltpu.SMEM)
HBM = pl.BlockSpec(memory_space=pltpu.HBM)
PARAMS = pltpu.CompilerParams(vmem_limit_bytes=40 * 1024 * 1024)


def shards(harmonics, noise_weight, order_table, curve_weight):
    ta_count = lax.axis_size("ta")
    ma_count = lax.axis_size("ma")
    noise = noise_weight.reshape(SIDE, SIDE)
    within = lax.ppermute(noise, "ma", [(i, i ^ 1) for i in range(ma_count)])
    across = lax.ppermute(noise, "ma", [(i, i + 1 if i % 2 else i - 1) for i in range(1, ma_count - 1)])
    packed = harmonics.reshape(2, 2, 64, SIDE).transpose(0, 2, 1, 3).reshape(2, SIDE, SIDE)
    square = jax.ShapeDtypeStruct((2 * CYCLES, SIDE), F32)
    orders_there = pltpu.with_memory_space_constraint(order_table, pltpu.HBM)
    packed = pltpu.with_memory_space_constraint(packed, pltpu.HBM)
    table, sent, order_rows, turns, basis, basis_turned, small = pl.pallas_call(
        legendre_kernel,
        in_specs=[HBM, HBM, HBM],
        out_specs=[VMEM] * 7,
        out_shape=[
            jax.ShapeDtypeStruct((SIDE, ROWS, SIDE), F32),
            square,
            jax.ShapeDtypeStruct((8, SIDE), jnp.int32),
            jax.ShapeDtypeStruct((2, SIDE, SIDE), F32),
            jax.ShapeDtypeStruct((SIDE, 2 * SIDE), BF16),
            jax.ShapeDtypeStruct((SIDE, 2 * SIDE), BF16),
            jax.ShapeDtypeStruct((3, 8, SIDE), F32),
        ],
        scratch_shapes=[
            pltpu.VMEM((SIDE, SIDE), F32),
            pltpu.VMEM((SIDE, SIDE), F32),
            pltpu.VMEM((4, SIDE, SIDE), F32),
            pltpu.SMEM((CYCLES,), jnp.int32),
            pltpu.VMEM((2, SIDE, SIDE), F32),
            pltpu.VMEM((1, CYCLES), jnp.int32),
            pltpu.SemaphoreType.DMA((3,)),
        ],
        compiler_params=PARAMS,
        name="legendre",
    )(orders_there, pltpu.with_memory_space_constraint(order_table.reshape(1, CYCLES), pltpu.HBM), packed)
    sent, within, across = lax.optimization_barrier((sent, within, across))
    received = lax.all_to_all(sent, "ma", split_axis=0, concat_axis=0, tiled=True)
    kappa, sent = pl.pallas_call(
        euler_kernel,
        in_specs=[HBM, VMEM, VMEM, VMEM, VMEM, VMEM, HBM, VMEM, VMEM],
        out_specs=[HBM, VMEM],
        out_shape=[jax.ShapeDtypeStruct((2, SIDE, SIDE), F32), square],
        scratch_shapes=[
            pltpu.VMEM((2, 7, SIDE, SIDE), F32),
            pltpu.VMEM((2 * LEVELS, 8, SIDE), F32),
            pltpu.SMEM((2, LEVELS), F32),
            pltpu.VMEM((SIDE, SIDE), F32),
            pltpu.VMEM((2, SIDE, SIDE), F32),
            pltpu.SemaphoreType.DMA((3,)),
        ],
        compiler_params=PARAMS,
        name="euler",
    )(
        pltpu.with_memory_space_constraint(curve_weight, pltpu.HBM),
        turns,
        basis,
        basis_turned,
        small,
        received,
        pltpu.with_memory_space_constraint(noise, pltpu.HBM),
        within, across)
    received = lax.all_to_all(sent, "ma", split_axis=0, concat_axis=0, tiled=True)
    counts = jnp.sum(received.reshape(CYCLES, 2, SIDE)[:, 0, CYCLES:], axis=0).reshape(2, LEVELS)
    one, two, three = [lax.ppermute(counts, "ta", [(i, i ^ by) for i in range(ta_count)]) for by in (1, 2, 3)]
    curve = ((counts + one) + (two + three)) / (ta_count * CYCLES * NPIX)
    gradient = pl.pallas_call(
        adjoint_kernel,
        in_specs=[VMEM, VMEM, VMEM],
        out_specs=VMEM,
        out_shape=jax.ShapeDtypeStruct((2, SIDE, SIDE), F32),
        scratch_shapes=[pltpu.VMEM((2, SIDE, SIDE), F32)],
        compiler_params=PARAMS,
        name="adjoint",
    )(order_rows, received, table)
    gradient = gradient.reshape(2, 64, 2, SIDE).transpose(0, 2, 1, 3).reshape(1, 2, 1, 2, LMAX)
    return kappa.reshape(1, 2, 1, NPIX), curve, gradient


def solution(mesh):
    in_specs = (P("ta", None, "ma", None, None), P("ta", "ma", None), P(), P())
    out_specs = (P("ta", None, "ma", None), P(), P("ta", None, "ma", None, None))
    return jax.shard_map(shards, mesh=mesh, in_specs=in_specs, out_specs=out_specs, check_vma=False)
```

time: 66.8 us -> 58.1 us (0.87)
  local copies, waits for them, and re-layouts: 3.81 us -> 0.08 us
  Pallas kernels: 15.4 us -> 12.7 us
  starting transfers between devices: 10.3 us -> 7.96 us
    unnamed x10 -> x0, local copies, waits for them, and re-layouts: 3.72 us -> none
    pallas_call x3, Pallas kernels: 15.4 us -> 12.7 us  [the longest x1 6.32 us: shards(): pl.pallas_call(euler_kernel, in_specs=[HBM, VMEM, VMEM, VMEM, VMEM, VMEM,...]
    ppermute x2, starting transfers between devices: 7.07 us -> 4.69 us  [the longest x1 4.6 us: shards(): lax.ppermute(noise, 'ma', [(i, i + 1 if i % 2 else i - 1) for i in range(...]
  transfers between devices with their start and end apart: 5 -> 5, of which waited for: 0 -> 1; matrix products, arithmetic and copies ran while one was open for 0% -> 0% of each run, Pallas kernels for 11% -> 11%
where the time goes in v1:
time: 58.1 us; the launch traced here: 57.9 us
  blocking collectives  35.3 us (61%)
  Pallas kernels  12.7 us (22%)
  starting transfers between devices  7.96 us (14%)
  other arithmetic  0.72 us (1%)
  between operations  0.68 us (1%)
    all_to_all x2, blocking collectives, shards(): lax.all_to_all(sent, 'ma', split_axis=0, concat_axis=0, tiled=True)  35.3 us
    pallas_call x1, Pallas kernels, shards(): pl.pallas_call(euler_kernel, in_specs=[HBM, VMEM, VMEM, VMEM, VMEM, VMEM,...  6.32 us
    ppermute x1, starting transfers between devices, shards(): lax.ppermute(noise, 'ma', [(i, i + 1 if i % 2 else i - 1) for i in range(...  4.6 us
    pallas_call x1, Pallas kernels, shards(): pl.pallas_call(legendre_kernel, in_specs=[HBM, HBM, HBM], out_specs=[VMEM...  3.73 us
    ppermute x3, starting transfers between devices, shards(): lax.ppermute(counts, 'ta', [(i, i ^ by) for i in range(ta_count)])  3.27 us
    pallas_call x1, Pallas kernels, shards(): pl.pallas_call(adjoint_kernel, in_specs=[VMEM, VMEM, VMEM], out_specs=VME...  2.68 us
  transfers between devices with their start and end apart: 5, of which 1 were waited for; matrix products, arithmetic and copies ran while one was open for 0% of the time, Pallas kernels for 11%

profile of v1, /device:TPU:1, one launch (start us, length us, event | category | flops | bytes accessed | tf_op | source)
XLA Modules:
  0.0 57.9 jit_solution(4127855119127589145)
XLA Ops:
  0.6 4.6 %collective-permute-start.1 = (f32[128,128]{1,0:T(8,128)}, f32[128,128]{1,0:T(8,128)S(1)}, u32[]{:S(2)}, u32[]{:S(2)}) collective-permute-start(f32[128,128]{1,0:T(8,128)} %bitcast.23), channel_id=1, source_target_pairs={{4,8},{8,4},{12,16},{16,12},{20,24},{24,20},{28,32},{32,28},{36,40... | collective-permute-start | bytes 196616 | tf_op jit(solution)/shard_map/ppermute | solution.py:416
  5.2 0.1 collective-permute-start
  5.3 3.7 %legendre.1 = (f32[128,24,128]{2,1,0:T(8,128)S(1)}, f32[128,128]{1,0:T(8,128)S(1)}, s32[8,128]{1,0:T(8,128)S(1)}, f32[2,128,128]{2,1,0:T(8,128)S(1)}, bf16[128,2...) custom-call(s32[64]{0:T(128)} %orders_in.1, s32[1,64]{1,0:T(1,128)} %bitcast.26, ...), custom_call_target="tpu_custom_call" | custom-call | tf_op jit(solution)/shard_map/legendre/pallas_call | solution.py:421
  9.1 0.0 collective-permute-done.1.across
  9.1 0.0 collective-permute-done.within
  9.1 21.7 %all_to_all.22 = f32[64,2,128]{2,1,0:T(2,128)S(1)} all-to-all(f32[64,2,128]{2,1,0:T(2,128)S(1)} %bitcast.19), channel_id=1, replica_groups=mesh['ma'=64,'ta'=4] {'ma'}, dimensions={0} | all-to-all | bytes 131072 | tf_op jit(solution)/shard_map/all_to_all | solution.py:447
  30.8 6.3 %euler.1 = (f32[2,128,128]{2,1,0:T(8,128)}, f32[128,128]{1,0:T(8,128)S(1)}) custom-call(f32[2,32]{1,0:T(2,128)} %weights_in.1, f32[2,128,128]{2,1,0:T(8,128)S(1)} %get-tuple-element.15.turns, bf16[128,256]{1,0:T(8,128)(2,1)S(1)} %get-tuple-element.16.basis, bf16[128,256]{1,0:T(8,128)(2,1)S(1)} %get-tuple-element.17.basis_turned, ...), custom_call_target="tpu_custom_call" | custom-call | tf_op jit(solution)/shard_map/euler/pallas_call | solution.py:448
  37.2 13.5 %all_to_all.23 = f32[64,2,128]{2,1,0:T(2,128)S(1)} all-to-all(f32[64,2,128]{2,1,0:T(2,128)S(1)} %bitcast.20), channel_id=1, replica_groups=mesh['ma'=64,'ta'=4] {'ma'}, dimensions={0} | all-to-all | bytes 131072 | tf_op jit(solution)/shard_map/all_to_all | solution.py:472
  50.7 0.1 slice_reduce_fusion
  50.8 0.1 reshape.41
  50.9 2.5 %collective-permute-start.4 = (f32[2,32]{1,0:T(2,128)S(1)}, f32[2,32]{1,0:T(2,128)S(1)}, u32[]{:S(2)}, u32[]{:S(2)}) collective-permute-start(f32[2,32]{1,0:T(2,128)S(1)} %reshape.41), channel_id=1, source_target_pairs={{0,3},{1,2},{2,1},{3,0},{4,7},{5,6},{6,5},{7,4},{8,11},{9,10},{10,... | collective-permute-start | bytes 776 | tf_op jit(solution)/shard_map/ppermute | solution.py:474
  53.4 0.5 collective-permute-start.3
  53.9 0.3 collective-permute-start.2
  54.2 2.7 %adjoint.1 = f32[2,128,128]{2,1,0:T(8,128)} custom-call(s32[8,128]{1,0:T(8,128)S(1)} %get-tuple-element.25.order_rows, f32[128,128]{1,0:T(8,128)S(1)} %bitcast.17, f32[128,24,128]{2,1,0:T(8,128)S(1)} %get-tuple-element.26.table), custom_call_target="tpu_custom_call" | custom-call | tf_op jit(solution)/shard_map/adjoint/pallas_call | solution.py:476
  56.9 0.0 collective-permute-done.4
  56.9 0.5 collective-permute-done.3
  57.3 0.0 collective-permute-done.2
  57.3 0.6 add_multiply_fusion
Async XLA Ops:
  0.6 8.4 %collective-permute-start.1 = (f32[128,128]{1,0:T(8,128)}, f32[128,128]{1,0:T(8,128)S(1)}, u32[]{:S(2)}, u32[]{:S(2)}) collective-permute-start(f32[128,128]{1,0:T(8,128)} %bitcast.23), channel_id=1, source_target_pairs={{4,8},{8,4},{12,16},{16,12},{20,24},{24,20},{28,32},{32,28},{36,40... | collective-permute-start | bytes 196616 | tf_op jit(solution)/shard_map/ppermute | solution.py:416
  5.2 3.9 %collective-permute-start = (f32[128,128]{1,0:T(8,128)}, f32[128,128]{1,0:T(8,128)S(1)}, u32[]{:S(2)}, u32[]{:S(2)}) collective-permute-start(f32[128,128]{1,0:T(8,128)} %bitcast.24), channel_id=1, source_target_pairs={{0,4},{4,0},{8,12},{12,8},{16,20},{20,16},{24,28},{28,24},{32,36},... | collective-permute-start | bytes 196616 | tf_op jit(solution)/shard_map/ppermute | solution.py:415
  50.9 6.0 %collective-permute-start.4 = (f32[2,32]{1,0:T(2,128)S(1)}, f32[2,32]{1,0:T(2,128)S(1)}, u32[]{:S(2)}, u32[]{:S(2)}) collective-permute-start(f32[2,32]{1,0:T(2,128)S(1)} %reshape.41), channel_id=1, source_target_pairs={{0,3},{1,2},{2,1},{3,0},{4,7},{5,6},{6,5},{7,4},{8,11},{9,10},{10,... | collective-permute-start | bytes 776 | tf_op jit(solution)/shard_map/ppermute | solution.py:474
  53.4 3.9 %collective-permute-start.3 = (f32[2,32]{1,0:T(2,128)S(1)}, f32[2,32]{1,0:T(2,128)S(1)}, u32[]{:S(2)}, u32[]{:S(2)}) collective-permute-start(f32[2,32]{1,0:T(2,128)S(1)} %reshape.41), channel_id=1, source_target_pairs={{0,2},{1,3},{2,0},{3,1},{4,6},{5,7},{6,4},{7,5},{8,10},{9,11},{10,... | collective-permute-start | bytes 776 | tf_op jit(solution)/shard_map/ppermute | solution.py:474
  53.9 3.4 %collective-permute-start.2 = (f32[2,32]{1,0:T(2,128)S(1)}, f32[2,32]{1,0:T(2,128)S(1)}, u32[]{:S(2)}, u32[]{:S(2)}) collective-permute-start(f32[2,32]{1,0:T(2,128)S(1)} %reshape.41), channel_id=1, source_target_pairs={{0,1},{1,0},{2,3},{3,2},{4,5},{5,4},{6,7},{7,6},{8,9},{9,8},{10,11... | collective-permute-start | bytes 776 | tf_op jit(solution)/shard_map/ppermute | solution.py:474

commit v2 on v1

--- a/solution.py
+++ b/solution.py
@@ -81,8 +81,9 @@
     small[2] = jnp.where(eight == 0, 1.0, 2.0)
 
 
-def legendre_kernel(orders_in, row_in, harmonics_in, table, sent, order_out, turns, basis, basis_turned, small_out,
-                    first, second, coefficients, orders, harmonics, orders_row, sems):
+def legendre_kernel(orders_in, row_in, harmonics_in, noise_in, weights_in, table, sent, order_out, turns, basis, basis_turned,
+                    small_out, noise, weights,
+                    first, second, coefficients, orders, harmonics, orders_row, picked, sems):
     ma = lax.axis_index("ma")
     fetch_orders = pltpu.make_async_copy(orders_in, orders, sems.at[0])
     fetch_harmonics = pltpu.make_async_copy(harmonics_in, harmonics, sems.at[1])
@@ -90,6 +91,24 @@
     fetch_orders.start()
     fetch_row.start()
     fetch_harmonics.start()
+    fetch_noise = pltpu.make_async_copy(noise_in, noise, sems.at[3])
+    fetch_weights = pltpu.make_async_copy(weights_in, weights, sems.at[4])
+    fetch_noise.start()
+    fetch_weights.start()
+    square = (SIDE, SIDE)
+    alike = ((iota(square, 0) & 1) == (iota(square, 1) & 1)).astype(BF16)
+    sel = (2 * CYCLES, 4 * ROWS)
+    column = iota(sel, 1)
+    in_half = (column >= 2 * ROWS).astype(jnp.int32)
+    column = column - 2 * ROWS * in_half
+    odd = (column >= ROWS).astype(jnp.int32)
+    picked[...] = selection(iota(sel, 0) >> 1, odd == 1, in_half, column - ROWS * odd).astype(BF16)
+    shape = (ROWS, SIDE)
+    row, half = iota(shape, 0), iota(shape, 1) & 1
+    held = slot_cycle(half, row)
+    z = jnp.where(held >= 0, 4.0 * (64.0 - 2.0 * held.astype(F32)) / (3.0 * NPIX), 0.0)
+    below_one = 1.0 - (1.0 - z * z)
+    log_term = -below_one * (1.0 + below_one * (0.5 + below_one * (1.0 / 3.0)))
     fetch_orders.wait()
     order = orders[ma]
     order_out[...] = jnp.full(order_out.shape, order, jnp.int32)
@@ -110,12 +129,6 @@
     moving = degree_index > 0
     first[...] = jnp.where(moving, alpha, 0.0)
     second[...] = jnp.where(moving, -alpha * beta, 1.0)
-    shape = (ROWS, SIDE)
-    row, half = iota(shape, 0), iota(shape, 1) & 1
-    held = slot_cycle(half, row)
-    z = jnp.where(held >= 0, 4.0 * (64.0 - 2.0 * held.astype(F32)) / (3.0 * NPIX), 0.0)
-    below_one = 1.0 - (1.0 - z * z)
-    log_term = -below_one * (1.0 + below_one * (0.5 + below_one * (1.0 / 3.0)))
     full = jnp.full(shape, order_value, F32)
     seed = jnp.exp(
         0.5 * jnp.log((2.0 * full + 1.0) / (4.0 * math.pi))
@@ -123,7 +136,7 @@
         + 0.5 * full * log_term
     )
 
-    unroll = 8
+    unroll = 16
 
     def compose(block, state):
         pu, pl_, qu, ql = state
@@ -176,7 +189,6 @@
     state = lax.fori_loop(0, SIDE // unroll, advance, (upper, lower) + (zeros,) * 8)
     sums = state[2:]
     high, low = split(jnp.concatenate(sums, axis=0))
-    alike = ((iota(square, 0) & 1) == (iota(square, 1) & 1)).astype(BF16)
     sums = mxu(jnp.concatenate([high, low], axis=1), jnp.concatenate([alike, alike], axis=0))
     small = (2 * ROWS, SIDE)
     pair, lane_half = iota(small, 1) >> 1, iota(small, 1) & 1
@@ -186,19 +198,15 @@
         held_sums = jnp.where(pair == f, jnp.concatenate(both, axis=0), held_sums)
     halves = jnp.concatenate([jnp.where(lane_half == half, held_sums, 0.0) for half in range(2)], axis=0)
     high, low = split(halves)
-    sel = (2 * CYCLES, 4 * ROWS)
-    at_row = iota(sel, 1)
-    in_half = (at_row >= 2 * ROWS).astype(jnp.int32)
-    at_row = at_row - 2 * ROWS * in_half
-    odd = (at_row >= ROWS).astype(jnp.int32)
-    pick = selection(iota(sel, 0) >> 1, odd == 1, in_half, at_row - ROWS * odd).astype(BF16)
-    own = mxu(jnp.concatenate([pick, pick], axis=1), jnp.concatenate([high, low], axis=0))
+    own = mxu(jnp.concatenate([picked[...], picked[...]], axis=1), jnp.concatenate([high, low], axis=0))
     even_lane = (iota(square, 1) & 1) == 0
     own = own + jnp.where(even_lane, pltpu.roll(own, SIDE - 1, 1), pltpu.roll(own, 1, 1))
     own = jnp.where(iota(square, 1) < 8, own, 0.0)
     before = pltpu.roll(own, 2, 0)
     after = pltpu.roll(own, 2 * CYCLES - 2, 0)
     sent[...] = own + pltpu.roll(before, 8, 1) + pltpu.roll(after, 16, 1)
+    fetch_noise.wait()
+    fetch_weights.wait()
 
 
 def both_halves(a, pair):
@@ -221,12 +229,8 @@
     return jnp.where(lane == 0, pltpu.roll(moved, 1, 0), moved)
 
 
-def euler_kernel(weights_in, turns, basis, basis_turned, small, received, noise_in, within, across, kappa_out, sent,
-                 fields, counts, level_weights, noise, kappa, sems):
-    fetch_weights = pltpu.make_async_copy(weights_in, level_weights, sems.at[0])
-    fetch_noise = pltpu.make_async_copy(noise_in, noise, sems.at[1])
-    fetch_weights.start()
-    fetch_noise.start()
+def euler_kernel(level_weights, turns, basis, basis_turned, small, received, noise, within, across, kappa_out, sent,
+                 fields, counts, kappa, sems):
     cycle = lax.axis_index("ma")
     parity = (cycle + 1 + NPIX // 4 - CYCLES // 2) % 2
     square = (SIDE, SIDE)
@@ -253,9 +257,8 @@
 
     for r in range(2):
         kappa[r] = maps[r * SIDE : (r + 1) * SIDE]
-    keep_kappa = pltpu.make_async_copy(kappa, kappa_out, sems.at[2])
+    keep_kappa = pltpu.make_async_copy(kappa, kappa_out, sems.at[0])
     keep_kappa.start()
-    fetch_noise.wait()
 
     second_of_chip = cycle % 2 == 1
     noise_before = jnp.where(second_of_chip, within[...], across[...])
@@ -286,29 +289,31 @@
         fields[r, 6] = jnp.where(odd, moved_above, above)
 
     counts[...] = jnp.zeros_like(counts)
-    fetch_weights.wait()
     def sweep(top):
-        for r in range(2):
-
-            def tile(index, carry, r=r):
-                at = pl.ds(pl.multiple_of(index * TILE, TILE), TILE)
-                held = [fields[r, n, at, :] for n in range(5 if top else 7)]
-                total = jnp.zeros((TILE, SIDE), F32)
-                for t in range(LEVELS):
-                    twice = 2.0 * (-3.0 + 6.0 * t / (LEVELS - 1))
-                    u, e, w, d, dd, *others = [jnp.tanh(x - twice) for x in held]
-                    n1, n2 = others if others else (-1.0, -1.0)
-                    down = dd * (d + e)
-                    up = 1.0 - e if top else n2 * (e + n1)
-                    inner = down + up + w * (d + n1) - 2.0
-                    scaled = level_weights[r, t] * u
-                    total = total + inner * (level_weights[r, t] - scaled * u)
-                    part = u * (2.0 - down - up) if top else u * (2.0 - down)
-                    counts[r * LEVELS + t] += jnp.sum(part.reshape(TILE // 8, 8, SIDE), axis=0)
-                fields[r, 0, at, :] = total
-                return carry
-
-            lax.fori_loop(0, SIDE // TILE, tile, 0)
+        def tile(index, r):
+            at = pl.ds(pl.multiple_of(index * TILE, TILE), TILE)
+            held = [fields[r, n, at, :] for n in range(5 if top else 7)]
+            total = jnp.zeros((TILE, SIDE), F32)
+            for t in range(LEVELS):
+                twice = 2.0 * (-3.0 + 6.0 * t / (LEVELS - 1))
+                u, e, w, d, dd, *others = [jnp.tanh(x - twice) for x in held]
+                n1, n2 = others if others else (-1.0, -1.0)
+                down = dd * (d + e)
+                up = 1.0 - e if top else n2 * (e + n1)
+                inner = down + up + w * (d + n1) - 2.0
+                scaled = level_weights[r, t] * u
+                total = total + inner * (level_weights[r, t] - scaled * u)
+                part = u * (2.0 - down - up) if top else u * (2.0 - down)
+                counts[r * LEVELS + t] += jnp.sum(part.reshape(TILE // 8, 8, SIDE), axis=0)
+            fields[r, 0, at, :] = total
+
+        def tiles(index, carry):
+            for more in range(1):
+                for r in range(2):
+                    tile(index * 1 + more, r)
+            return carry
+
+        lax.fori_loop(0, SIDE // TILE // 1, tiles, 0)
 
     pl.when(cycle == 0)(lambda: sweep(True))
     pl.when(cycle > 0)(lambda: sweep(False))
@@ -378,25 +383,31 @@
 
     even_lane = (iota((8, SIDE), 1) & 1) == 0
 
-    def block(index, carry):
+    def block(index):
         at = pl.ds(pl.multiple_of(index * 8, 8), 8)
-        values = [table[index * 8 + s] for s in range(8)]
+        held = {}
+        for s in range(8):
+            value = table[index * 8 + s]
+            for r in range(2):
+                for kind in range(2):
+                    product = value * factors[s % 2][r][kind]
+                    part = product[:8] + product[8:16] + product[16:]
+                    by = 1
+                    while s & by:
+                        part = merge(held.pop((r, kind, by)), part, by)
+                        by *= 2
+                    held[r, kind, by] = part
         for r in range(2):
-            summed = []
-            for kind in range(2):
-                parts = []
-                for s in range(8):
-                    product = values[s] * factors[s % 2][r][kind]
-                    parts.append(product[:8] + product[8:16] + product[16:])
-                for by in (1, 2, 4):
-                    parts = [merge(a, b, by) for a, b in zip(parts[::2], parts[1::2])]
-                summed.append(parts[0])
-            straight, crossed = summed
+            straight, crossed = held[r, 0, 8], held[r, 1, 8]
             crossed = jnp.where(even_lane, pltpu.roll(crossed, SIDE - 1, 1), pltpu.roll(crossed, 1, 1))
             turned[r, at, :] = straight + crossed
+
+    def blocks(index, carry):
+        for more in range(4):
+            block(index * 4 + more)
         return carry
 
-    lax.fori_loop(0, SIDE // 8, block, 0)
+    lax.fori_loop(0, SIDE // 8 // 4, blocks, 0)
     for r in range(2):
         degree_index = (row >> 1) * SIDE + lane
         gradient[r] = jnp.where(degree_index < LMAX - order, turned[r].T, 0.0)
@@ -418,10 +429,10 @@
     square = jax.ShapeDtypeStruct((2 * CYCLES, SIDE), F32)
     orders_there = pltpu.with_memory_space_constraint(order_table, pltpu.HBM)
     packed = pltpu.with_memory_space_constraint(packed, pltpu.HBM)
-    table, sent, order_rows, turns, basis, basis_turned, small = pl.pallas_call(
+    table, sent, order_rows, turns, basis, basis_turned, small, noise_here, weights = pl.pallas_call(
         legendre_kernel,
-        in_specs=[HBM, HBM, HBM],
-        out_specs=[VMEM] * 7,
+        in_specs=[HBM] * 5,
+        out_specs=[VMEM] * 9,
         out_shape=[
             jax.ShapeDtypeStruct((SIDE, ROWS, SIDE), F32),
             square,
@@ -430,6 +441,8 @@
             jax.ShapeDtypeStruct((SIDE, 2 * SIDE), BF16),
             jax.ShapeDtypeStruct((SIDE, 2 * SIDE), BF16),
             jax.ShapeDtypeStruct((3, 8, SIDE), F32),
+            jax.ShapeDtypeStruct((SIDE, SIDE), F32),
+            jax.ShapeDtypeStruct((2, LEVELS), F32),
         ],
         scratch_shapes=[
             pltpu.VMEM((SIDE, SIDE), F32),
@@ -438,37 +451,44 @@
             pltpu.SMEM((CYCLES,), jnp.int32),
             pltpu.VMEM((2, SIDE, SIDE), F32),
             pltpu.VMEM((1, CYCLES), jnp.int32),
-            pltpu.SemaphoreType.DMA((3,)),
+            pltpu.VMEM((2 * CYCLES, 4 * ROWS), BF16),
+            pltpu.SemaphoreType.DMA((5,)),
         ],
         compiler_params=PARAMS,
         name="legendre",
-    )(orders_there, pltpu.with_memory_space_constraint(order_table.reshape(1, CYCLES), pltpu.HBM), packed)
+    )(
+        orders_there,
+        pltpu.with_memory_space_constraint(order_table.reshape(1, CYCLES), pltpu.HBM),
+        packed,
+        pltpu.with_memory_space_constraint(noise, pltpu.HBM),
+        pltpu.with_memory_space_constraint(curve_weight, pltpu.HBM),
+    )
     sent, within, across = lax.optimization_barrier((sent, within, across))
     received = lax.all_to_all(sent, "ma", split_axis=0, concat_axis=0, tiled=True)
     kappa, sent = pl.pallas_call(
         euler_kernel,
-        in_specs=[HBM, VMEM, VMEM, VMEM, VMEM, VMEM, HBM, VMEM, VMEM],
+        in_specs=[SMEM] + [VMEM] * 8,
         out_specs=[HBM, VMEM],
         out_shape=[jax.ShapeDtypeStruct((2, SIDE, SIDE), F32), square],
         scratch_shapes=[
             pltpu.VMEM((2, 7, SIDE, SIDE), F32),
             pltpu.VMEM((2 * LEVELS, 8, SIDE), F32),
-            pltpu.SMEM((2, LEVELS), F32),
-            pltpu.VMEM((SIDE, SIDE), F32),
             pltpu.VMEM((2, SIDE, SIDE), F32),
-            pltpu.SemaphoreType.DMA((3,)),
+            pltpu.SemaphoreType.DMA((1,)),
         ],
         compiler_params=PARAMS,
         name="euler",
     )(
-        pltpu.with_memory_space_constraint(curve_weight, pltpu.HBM),
+        weights,
         turns,
         basis,
         basis_turned,
         small,
         received,
-        pltpu.with_memory_space_constraint(noise, pltpu.HBM),
-        within, across)
+        noise_here,
+        within,
+        across,
+    )
     received = lax.all_to_all(sent, "ma", split_axis=0, concat_axis=0, tiled=True)
     counts = jnp.sum(received.reshape(CYCLES, 2, SIDE)[:, 0, CYCLES:], axis=0).reshape(2, LEVELS)
     one, two, three = [lax.ppermute(counts, "ta", [(i, i ^ by) for i in range(ta_count)]) for by in (1, 2, 3)]

time: 58.1 us -> 57.7 us (level)
  Pallas kernels: 12.7 us -> 11.3 us
  waiting for transfers between devices: 0.47 us -> 1.41 us
    ppermute x3, waiting for transfers between devices: 0.47 us -> 1.41 us  [shards(): lax.ppermute(counts, 'ta', [(i, i ^ by) for i in range(ta_count)])]
    pallas_call x1, Pallas kernels: 2.68 us -> 1.74 us  [shards(): pl.pallas_call(adjoint_kernel, in_specs=[VMEM, VMEM, VMEM], out_specs=VME...]
  transfers between devices with their start and end apart: 5 -> 5, of which waited for: 1 -> 1; matrix products, arithmetic and copies ran while one was open for 0% -> 0% of each run, Pallas kernels for 11% -> 9%
where the time goes in v2:
time: 57.7 us; the launch traced here: 57.5 us
  blocking collectives  35.4 us (61%)
  Pallas kernels  11.3 us (20%)
  starting transfers between devices  7.95 us (14%)
  waiting for transfers between devices  1.41 us (2%)
  other arithmetic  0.72 us (1%)
  between operations  0.68 us (1%)
    all_to_all x2, blocking collectives, shards(): lax.all_to_all(sent, 'ma', split_axis=0, concat_axis=0, tiled=True)  35.4 us
    pallas_call x1, Pallas kernels, shards(): pl.pallas_call(euler_kernel, in_specs=[SMEM] + [VMEM] * 8, out_specs=[HBM...  5.9 us
    ppermute x1, starting transfers between devices, shards(): lax.ppermute(noise, 'ma', [(i, i + 1 if i % 2 else i - 1) for i in range(...  4.59 us
    pallas_call x1, Pallas kernels, shards(): pl.pallas_call(legendre_kernel, in_specs=[HBM] * 5, out_specs=[VMEM] * 9,...  3.63 us
    ppermute x3, starting transfers between devices, shards(): lax.ppermute(counts, 'ta', [(i, i ^ by) for i in range(ta_count)])  3.27 us
    pallas_call x1, Pallas kernels, shards(): pl.pallas_call(adjoint_kernel, in_specs=[VMEM, VMEM, VMEM], out_specs=VME...  1.74 us
    ppermute x3, waiting for transfers between devices, shards(): lax.ppermute(counts, 'ta', [(i, i ^ by) for i in range(ta_count)])  1.41 us
  transfers between devices with their start and end apart: 5, of which 1 were waited for; matrix products, arithmetic and copies ran while one was open for 0% of the time, Pallas kernels for 9%

profile of v2, /device:TPU:1, one launch (start us, length us, event | category | flops | bytes accessed | tf_op | source)
XLA Modules:
  0.0 57.5 jit_solution(7521556846564999592)
XLA Ops:
  0.6 4.6 %collective-permute-start.1 = (f32[128,128]{1,0:T(8,128)}, f32[128,128]{1,0:T(8,128)S(1)}, u32[]{:S(2)}, u32[]{:S(2)}) collective-permute-start(f32[128,128]{1,0:T(8,128)} %bitcast.23), channel_id=1, source_target_pairs={{4,8},{8,4},{12,16},{16,12},{20,24},{24,20},{28,32},{32,28},{36,40... | collective-permute-start | bytes 196616 | tf_op jit(solution)/shard_map/ppermute | solution.py:427
  5.2 0.1 collective-permute-start
  5.3 3.6 %legendre.1 = (f32[128,24,128]{2,1,0:T(8,128)S(1)}, f32[128,128]{1,0:T(8,128)S(1)}, s32[8,128]{1,0:T(8,128)S(1)}, f32[2,128,128]{2,1,0:T(8,128)S(1)}, bf16[128,2...) custom-call(s32[64]{0:T(128)} %orders_in.1, ...), custom_call_target="tpu_custom_call" | custom-call | tf_op jit(solution)/shard_map/legendre/pallas_call | solution.py:432
  9.0 0.0 collective-permute-done.1.across
  9.0 0.0 collective-permute-done.within
  9.0 21.8 %all_to_all.22 = f32[64,2,128]{2,1,0:T(2,128)S(1)} all-to-all(f32[64,2,128]{2,1,0:T(2,128)S(1)} %bitcast.19), channel_id=1, replica_groups=mesh['ma'=64,'ta'=4] {'ma'}, dimensions={0} | all-to-all | bytes 131072 | tf_op jit(solution)/shard_map/all_to_all | solution.py:467
  30.8 5.9 %euler.1 = (f32[2,128,128]{2,1,0:T(8,128)}, f32[128,128]{1,0:T(8,128)S(1)}) custom-call(f32[2,32]{1,0:T(2,128)S(1)} %get-tuple-element.17.level_weights, f32[2,128,128]{2,1,0:T(8,128)S(1)} %get-tuple-element.18.turns, bf16[128,256]{1,0:T(8,128)(2,1)S(1)} %get-tuple-element.19.basis, bf16[128,256]{1,0:T(8,128)(2,1)S(1)} %get-tuple-element.20.basis_turned, ...), custom_call_target="tpu_custom_call" | custom-call | tf_op jit(solution)/shard_map/euler/pallas_call | solution.py:468
  36.7 13.5 %all_to_all.23 = f32[64,2,128]{2,1,0:T(2,128)S(1)} all-to-all(f32[64,2,128]{2,1,0:T(2,128)S(1)} %bitcast.20), channel_id=1, replica_groups=mesh['ma'=64,'ta'=4] {'ma'}, dimensions={0} | all-to-all | bytes 131072 | tf_op jit(solution)/shard_map/all_to_all | solution.py:492
  50.3 0.1 slice_reduce_fusion
  50.4 0.1 reshape.41
  50.5 2.5 %collective-permute-start.4 = (f32[2,32]{1,0:T(2,128)S(1)}, f32[2,32]{1,0:T(2,128)S(1)}, u32[]{:S(2)}, u32[]{:S(2)}) collective-permute-start(f32[2,32]{1,0:T(2,128)S(1)} %reshape.41), channel_id=1, source_target_pairs={{0,3},{1,2},{2,1},{3,0},{4,7},{5,6},{6,5},{7,4},{8,11},{9,10},{10,... | collective-permute-start | bytes 776 | tf_op jit(solution)/shard_map/ppermute | solution.py:494
  53.0 0.5 collective-permute-start.3
  53.5 0.3 collective-permute-start.2
  53.8 1.7 %adjoint.1 = f32[2,128,128]{2,1,0:T(8,128)} custom-call(s32[8,128]{1,0:T(8,128)S(1)} %get-tuple-element.29.order_rows, f32[128,128]{1,0:T(8,128)S(1)} %bitcast.17, f32[128,24,128]{2,1,0:T(8,128)S(1)} %get-tuple-element.30.table), custom_call_target="tpu_custom_call" | custom-call | tf_op jit(solution)/shard_map/adjoint/pallas_call | solution.py:496
  55.5 0.0 collective-permute-done.4
  55.5 1.4 %collective-permute-done.3 = f32[2,32]{1,0:T(2,128)S(1)} collective-permute-done((f32[2,32]{1,0:T(2,128)S(1)}, f32[2,32]{1,0:T(2,128)S(1)}, u32[]{:S(2)}, u32[]{:S(2)}) %collective-permute-start.3) | collective-permute-done | bytes 288 | tf_op jit(solution)/shard_map/ppermute | solution.py:494
  56.9 0.0 collective-permute-done.2
  56.9 0.6 add_multiply_fusion
Async XLA Ops:
  0.6 8.3 %collective-permute-start.1 = (f32[128,128]{1,0:T(8,128)}, f32[128,128]{1,0:T(8,128)S(1)}, u32[]{:S(2)}, u32[]{:S(2)}) collective-permute-start(f32[128,128]{1,0:T(8,128)} %bitcast.23), channel_id=1, source_target_pairs={{4,8},{8,4},{12,16},{16,12},{20,24},{24,20},{28,32},{32,28},{36,40... | collective-permute-start | bytes 196616 | tf_op jit(solution)/shard_map/ppermute | solution.py:427
  5.2 3.8 %collective-permute-start = (f32[128,128]{1,0:T(8,128)}, f32[128,128]{1,0:T(8,128)S(1)}, u32[]{:S(2)}, u32[]{:S(2)}) collective-permute-start(f32[128,128]{1,0:T(8,128)} %bitcast.24), channel_id=1, source_target_pairs={{0,4},{4,0},{8,12},{12,8},{16,20},{20,16},{24,28},{28,24},{32,36},... | collective-permute-start | bytes 196616 | tf_op jit(solution)/shard_map/ppermute | solution.py:426
  50.5 5.0 %collective-permute-start.4 = (f32[2,32]{1,0:T(2,128)S(1)}, f32[2,32]{1,0:T(2,128)S(1)}, u32[]{:S(2)}, u32[]{:S(2)}) collective-permute-start(f32[2,32]{1,0:T(2,128)S(1)} %reshape.41), channel_id=1, source_target_pairs={{0,3},{1,2},{2,1},{3,0},{4,7},{5,6},{6,5},{7,4},{8,11},{9,10},{10,... | collective-permute-start | bytes 776 | tf_op jit(solution)/shard_map/ppermute | solution.py:494
  53.0 3.9 %collective-permute-start.3 = (f32[2,32]{1,0:T(2,128)S(1)}, f32[2,32]{1,0:T(2,128)S(1)}, u32[]{:S(2)}, u32[]{:S(2)}) collective-permute-start(f32[2,32]{1,0:T(2,128)S(1)} %reshape.41), channel_id=1, source_target_pairs={{0,2},{1,3},{2,0},{3,1},{4,6},{5,7},{6,4},{7,5},{8,10},{9,11},{10,... | collective-permute-start | bytes 776 | tf_op jit(solution)/shard_map/ppermute | solution.py:494
  53.5 3.4 %collective-permute-start.2 = (f32[2,32]{1,0:T(2,128)S(1)}, f32[2,32]{1,0:T(2,128)S(1)}, u32[]{:S(2)}, u32[]{:S(2)}) collective-permute-start(f32[2,32]{1,0:T(2,128)S(1)} %reshape.41), channel_id=1, source_target_pairs={{0,1},{1,0},{2,3},{3,2},{4,5},{5,4},{6,7},{7,6},{8,9},{9,8},{10,11... | collective-permute-start | bytes 776 | tf_op jit(solution)/shard_map/ppermute | solution.py:494

commit v3 on v2

--- a/solution.py
+++ b/solution.py
@@ -16,7 +16,7 @@
 LEVELS = 32
 SIDE = 128
 ROWS = 24
-TILE = 16
+GROUP = 4
 FAR = -1.0e9
 
 
@@ -72,13 +72,15 @@
     eight = jnp.broadcast_to(orders_row[...].astype(F32), (8, CYCLES))
     eight = dot(eight, twice.astype(F32), (1, 0)).astype(jnp.int32)
     orders = jnp.broadcast_to(eight[:1], square)
-    turns[0], turns[1] = turn_cos_sin(orders * row, SIDE)
-    cosine, sine = turn_cos_sin(orders * row, NPIX)
+    down = orders.astype(F32).T.astype(jnp.int32)
+    turns[0], turns[1] = turn_cos_sin(down * lane, SIDE)
+    pixel = 16 * (row & 7) + (row >> 3)
+    cosine, sine = turn_cos_sin(orders * pixel, NPIX)
     turned = jnp.where((lane & 1) == 0, cosine, sine)
     for ref, value in ((basis, turned.T), (basis_turned, turned)):
         ref[:, :SIDE], ref[:, SIDE:] = split(value)
-    small[0], small[1] = turn_cos_sin(eight, 2 * NPIX)
-    small[2] = jnp.where(eight == 0, 1.0, 2.0)
+    small[0], small[1] = turn_cos_sin(down, 2 * NPIX)
+    small[2] = jnp.where(down == 0, 1.0, 2.0)
 
 
 def legendre_kernel(orders_in, row_in, harmonics_in, noise_in, weights_in, table, sent, order_out, turns, basis, basis_turned,
@@ -209,132 +211,136 @@
     fetch_weights.wait()
 
 
-def both_halves(a, pair):
-    product = mxu(jnp.concatenate(split(a), axis=1), jnp.concatenate([pair, pair], axis=0))
-    return product[:, :SIDE] + product[:, SIDE:]
-
-
-def swapped(x):
-    x = jnp.broadcast_to(x, (8, SIDE))
-    even = (iota((8, SIDE), 1) & 1) == 0
-    return jnp.where(even, pltpu.roll(x, SIDE - 1, 1), pltpu.roll(x, 1, 1))[:1]
-
-
-def neighbour(x, by):
-    lane = iota((SIDE, SIDE), 1)
-    if by == 1:
-        moved = pltpu.roll(x, SIDE - 1, 1)
-        return jnp.where(lane == SIDE - 1, pltpu.roll(moved, SIDE - 1, 0), moved)
-    moved = pltpu.roll(x, 1, 1)
-    return jnp.where(lane == 0, pltpu.roll(moved, 1, 0), moved)
+def both_halves(pair, b):
+    high, low = pair[:, :SIDE], pair[:, SIDE:]
+    left = jnp.concatenate([jnp.concatenate([high, high], axis=1), jnp.concatenate([low, low], axis=1)], axis=0)
+    product = mxu(left, jnp.concatenate(split(b), axis=0))
+    return product[:SIDE] + product[SIDE:]
+
+
+def row_pairs_swapped(x):
+    even = (iota((SIDE, SIDE), 0) & 1) == 0
+    return jnp.where(even, pltpu.roll(x, SIDE - 1, 0), pltpu.roll(x, 1, 0))
 
 
 def euler_kernel(level_weights, turns, basis, basis_turned, small, received, noise, within, across, kappa_out, sent,
-                 fields, counts, kappa, sems):
+                 fields, counts, kappa, gradients, flips, sems):
     cycle = lax.axis_index("ma")
     parity = (cycle + 1 + NPIX // 4 - CYCLES // 2) % 2
     square = (SIDE, SIDE)
-    row = iota(square, 0)
+    lane, row = iota(square, 1), iota(square, 0)
+    real_row = (row & 1) == 0
     a_cos, a_sin = turns[0], turns[1]
-    spin_cos, spin_sin, weight = small[0, :1], small[1, :1], small[2, :1]
-    low = (iota((1, SIDE), 1) & 1) == 0
-
-    flipped = received[...].T
+    spin_cos, spin_sin, weight = small[0], small[1], small[2]
+
+    arrived = received[...]
+    real_lane = ((lane >> 1) & 1) == 0
+    partner = jnp.where(real_lane, pltpu.roll(arrived, SIDE - 2, 1), pltpu.roll(arrived, 2, 1))
+    turned = (lane < 8) == (parity == 1)
+    cs = jnp.where(turned, spin_cos, 1.0)
+    sn = jnp.where(turned, spin_sin, 0.0)
+    spun = weight * (arrived * cs + jnp.where(real_lane, -partner, partner) * sn)
     lefts = []
     for kk in range(3):
-        turned = parity == 1 if kk == 0 else parity == 0
-        cs = jnp.where(turned, spin_cos, 1.0)
-        sn = jnp.where(turned, spin_sin, 0.0)
         for r in range(2):
-            real = flipped[8 * kk + 4 * r : 8 * kk + 4 * r + 1]
-            imag = flipped[8 * kk + 4 * r + 2 : 8 * kk + 4 * r + 3]
-            c_real = weight * (real * cs - imag * sn)
-            c_imag = weight * (real * sn + imag * cs)
-            u = jnp.where(low, c_real, -c_imag)
-            v = jnp.where(low, -c_imag, -c_real)
-            lefts.append(u * a_cos + v * a_sin)
-    maps = both_halves(jnp.concatenate(lefts, axis=0), basis[...])
+            at = 8 * kk + 4 * r
+            real = jnp.broadcast_to(spun[:, at : at + 1], square)
+            imag = jnp.broadcast_to(spun[:, at + 2 : at + 3], square)
+            lefts.append(jnp.where(real_row, real, -imag) * a_cos - jnp.where(real_row, imag, real) * a_sin)
+    maps = both_halves(basis_turned[...], jnp.concatenate(lefts, axis=1))
 
     for r in range(2):
-        kappa[r] = maps[r * SIDE : (r + 1) * SIDE]
+        for v in range(16):
+            flips[r, pl.ds(v, 8, stride=16), :] = maps[8 * v : 8 * v + 8, r * SIDE : (r + 1) * SIDE]
+        kappa[r] = flips[r].T
     keep_kappa = pltpu.make_async_copy(kappa, kappa_out, sems.at[0])
     keep_kappa.start()
 
+    def arranged(x, slot):
+        flips[slot] = x.T
+        return jnp.concatenate([flips[slot, pl.ds(v, 8, stride=16), :] for v in range(16)], axis=0)
+
+    own_noise = arranged(noise[...], 2)
+    within_noise, across_noise = arranged(within[...], 3), arranged(across[...], 4)
     second_of_chip = cycle % 2 == 1
-    noise_before = jnp.where(second_of_chip, within[...], across[...])
-    noise_after = jnp.where(second_of_chip, across[...], within[...])
+    noise_before = jnp.where(second_of_chip, within_noise, across_noise)
+    noise_after = jnp.where(second_of_chip, across_noise, within_noise)
+    sub = iota((8, SIDE), 0)
 
     def ratio(kk, r, weights):
-        return 2.0 * (maps[(2 * kk + r) * SIDE : (2 * kk + r + 1) * SIDE] * weights)
-
-    odd = parity == 1
-
-    def aside(x):
-        by = jnp.where(odd, SIDE - 1, 1)
-        moved = pltpu.roll(x, by, 1)
-        edge = jnp.where(odd, SIDE - 1, 0)
-        return jnp.where(iota(square, 1) == edge, pltpu.roll(moved, by, 0), moved)
+        return 2.0 * (maps[:, (2 * kk + r) * SIDE : (2 * kk + r + 1) * SIDE] * weights)
 
     for r in range(2):
-        here = ratio(0, r, noise[...])
+        here = ratio(0, r, own_noise)
         above = jnp.where(cycle > 0, ratio(1, r, noise_before), FAR)
         below = jnp.where(cycle < CYCLES - 1, ratio(2, r, noise_after), FAR)
-        fields[r, 0] = here
-        fields[r, 1] = neighbour(here, 1)
-        fields[r, 2] = neighbour(here, -1)
-        moved_below, moved_above = aside(below), aside(above)
-        fields[r, 3] = jnp.where(odd, below, moved_below)
-        fields[r, 4] = jnp.where(odd, moved_below, below)
-        fields[r, 5] = jnp.where(odd, above, moved_above)
-        fields[r, 6] = jnp.where(odd, moved_above, above)
-
-    counts[...] = jnp.zeros_like(counts)
-    def sweep(top):
-        def tile(index, r):
-            at = pl.ds(pl.multiple_of(index * TILE, TILE), TILE)
-            held = [fields[r, n, at, :] for n in range(5 if top else 7)]
-            total = jnp.zeros((TILE, SIDE), F32)
-            for t in range(LEVELS):
-                twice = 2.0 * (-3.0 + 6.0 * t / (LEVELS - 1))
-                u, e, w, d, dd, *others = [jnp.tanh(x - twice) for x in held]
-                n1, n2 = others if others else (-1.0, -1.0)
-                down = dd * (d + e)
-                up = 1.0 - e if top else n2 * (e + n1)
+        for n, x in enumerate((here, below, above)):
+            fields[r, n, 8 : 8 + SIDE, :] = x
+            last = pltpu.roll(x[SIDE - 8 :], 1, 0)
+            fields[r, n, :8, :] = jnp.where(sub == 0, pltpu.roll(last, 1, 1), last)
+            first = pltpu.roll(x[:8], 7, 0)
+            fields[r, n, 8 + SIDE :, :] = jnp.where(sub == 7, pltpu.roll(first, SIDE - 1, 1), first)
+    gradients[...] = jnp.zeros_like(gradients)
+
+    def levels(r, group, odd, top):
+        held = range(GROUP)
+        number = [group * GROUP + g for g in held]
+        twice = [t.astype(F32) * (12.0 / (LEVELS - 1)) - 6.0 for t in number]
+        given = [level_weights[r, t] for t in number]
+        known = {}
+
+        def soft(n, v):
+            if (n, v) not in known:
+                x = fields[r, n, 8 * v + 8 : 8 * v + 16, :]
+                known[n, v] = [jnp.tanh(x - twice[g]) for g in held]
+            return known[n, v]
+
+        totals = [jnp.zeros((8, SIDE), F32)] * GROUP
+        for v in range(16):
+            ahead, behind = (v + 1, v - 1) if odd else (v - 1, v + 1)
+            slope = None
+            for g in held:
+                u, e, w, d = soft(0, v)[g], soft(0, ahead)[g], soft(0, behind)[g], soft(1, v)[g]
+                n1 = -1.0 if top else soft(2, v)[g]
+                down = soft(1, ahead)[g] * (d + e)
+                up = 1.0 - e if top else soft(2, ahead)[g] * (e + n1)
                 inner = down + up + w * (d + n1) - 2.0
-                scaled = level_weights[r, t] * u
-                total = total + inner * (level_weights[r, t] - scaled * u)
-                part = u * (2.0 - down - up) if top else u * (2.0 - down)
-                counts[r * LEVELS + t] += jnp.sum(part.reshape(TILE // 8, 8, SIDE), axis=0)
-            fields[r, 0, at, :] = total
-
-        def tiles(index, carry):
-            for more in range(1):
-                for r in range(2):
-                    tile(index * 1 + more, r)
+                part = inner * (given[g] - (given[g] * u) * u)
+                slope = part if slope is None else slope + part
+                totals[g] = totals[g] + (u * (2.0 - down - up) if top else u * (2.0 - down))
+            gradients[r, 8 * v : 8 * v + 8, :] += slope
+        for g in held:
+            counts[r * LEVELS + number[g]] = totals[g]
+
+    def sweep(odd, top):
+        def step(group, carry):
+            for r in range(2):
+                levels(r, group, odd, top)
             return carry
 
-        lax.fori_loop(0, SIDE // TILE // 1, tiles, 0)
-
-    pl.when(cycle == 0)(lambda: sweep(True))
-    pl.when(cycle > 0)(lambda: sweep(False))
+        lax.fori_loop(0, LEVELS // GROUP, step, 0)
+
+    pl.when(cycle == 0)(lambda: sweep(True, True))
+    pl.when((cycle > 0) & (parity == 1))(lambda: sweep(True, False))
+    pl.when(parity == 0)(lambda: sweep(False, False))
 
     scale = 1.0 / (4.0 * math.sqrt(CYCLES * NPIX))
-    duals = []
-    gradients = jnp.concatenate([fields[r, 0] * (noise[...] * scale) for r in range(2)], axis=0)
-    all_sums = both_halves(gradients, basis_turned[...])
+    back = both_halves(basis[...], jnp.concatenate([gradients[r] * (own_noise * scale) for r in range(2)], axis=1))
+    pieces = []
     for r in range(2):
-        sums = all_sums[r * SIDE : (r + 1) * SIDE]
-        near = jnp.sum(sums * a_cos, axis=0, keepdims=True)
-        far = jnp.sum(sums * a_sin, axis=0, keepdims=True)
-        far = swapped(far)
-        both = near + jnp.where(low, -far, far)
-        other = swapped(both)
-        cs = jnp.where(parity == 1, spin_cos, 1.0)
-        sn = jnp.where(parity == 1, spin_sin, 0.0)
-        duals.append(
-            weight * jnp.where(low, both * cs - other * sn, -(both * cs + other * sn))
-        )
-    stacked = jnp.where(row == 0, duals[0], jnp.where(row == 1, duals[1], 0.0)).T
+        sums = back[:, r * SIDE : (r + 1) * SIDE]
+        pieces += [sums * a_cos, sums * a_sin]
+    high, low = split(jnp.concatenate(pieces, axis=1))
+    piece, to = iota((4 * SIDE, SIDE), 0) >> 7, iota((4 * SIDE, SIDE), 1)
+    gather = (to == (piece >> 1) + 2 * (piece & 1)).astype(BF16)
+    near = mxu(high, gather) + mxu(low, gather)
+    far = pltpu.roll(row_pairs_swapped(near), SIDE - 2, 1)
+    both = near + jnp.where(real_row, -far, far)
+    other = row_pairs_swapped(both)
+    cs = jnp.where(parity == 1, spin_cos, 1.0)
+    sn = jnp.where(parity == 1, spin_sin, 0.0)
+    dual = weight * jnp.where(real_row, both * cs - other * sn, -(both * cs + other * sn))
+    stacked = jnp.where(lane < 2, dual, 0.0)
     level_sums = jnp.sum(counts[...], axis=1) * -0.125
     level_sums = level_sums + jnp.where(cycle == 0, 2.0 * NPIX / 8.0 / SIDE, 0.0)
     padded = jnp.concatenate([jnp.zeros_like(level_sums), level_sums], axis=0)
@@ -440,7 +446,7 @@
             jax.ShapeDtypeStruct((2, SIDE, SIDE), F32),
             jax.ShapeDtypeStruct((SIDE, 2 * SIDE), BF16),
             jax.ShapeDtypeStruct((SIDE, 2 * SIDE), BF16),
-            jax.ShapeDtypeStruct((3, 8, SIDE), F32),
+            jax.ShapeDtypeStruct((3, SIDE, SIDE), F32),
             jax.ShapeDtypeStruct((SIDE, SIDE), F32),
             jax.ShapeDtypeStruct((2, LEVELS), F32),
         ],
@@ -471,9 +477,11 @@
         out_specs=[HBM, VMEM],
         out_shape=[jax.ShapeDtypeStruct((2, SIDE, SIDE), F32), square],
         scratch_shapes=[
-            pltpu.VMEM((2, 7, SIDE, SIDE), F32),
+            pltpu.VMEM((2, 3, SIDE + 16, SIDE), F32),
             pltpu.VMEM((2 * LEVELS, 8, SIDE), F32),
             pltpu.VMEM((2, SIDE, SIDE), F32),
+            pltpu.VMEM((2, SIDE, SIDE), F32),
+            pltpu.VMEM((5, SIDE, SIDE), F32),
             pltpu.SemaphoreType.DMA((1,)),
         ],
         compiler_params=PARAMS,

time: 57.7 us -> 57.1 us (0.990)
  Pallas kernels: 11.3 us -> 10.6 us
    pallas_call x1, Pallas kernels: 5.9 us -> 5.25 us  [shards(): pl.pallas_call(euler_kernel, in_specs=[SMEM] + [VMEM] * 8, out_specs=[HBM...]
where the time goes in v3:
time: 57.1 us; the launch traced here: 56.9 us
  blocking collectives  35.4 us (62%)
  Pallas kernels  10.6 us (19%)
  starting transfers between devices  7.95 us (14%)
  waiting for transfers between devices  1.41 us (2%)
  other arithmetic  0.72 us (1%)
  between operations  0.68 us (1%)
    all_to_all x2, blocking collectives, shards(): lax.all_to_all(sent, 'ma', split_axis=0, concat_axis=0, tiled=True)  35.4 us
    pallas_call x1, Pallas kernels, shards(): pl.pallas_call(euler_kernel, in_specs=[SMEM] + [VMEM] * 8, out_specs=[HBM...  5.25 us
    ppermute x1, starting transfers between devices, shards(): lax.ppermute(noise, 'ma', [(i, i + 1 if i % 2 else i - 1) for i in range(...  4.59 us
    pallas_call x1, Pallas kernels, shards(): pl.pallas_call(legendre_kernel, in_specs=[HBM] * 5, out_specs=[VMEM] * 9,...  3.65 us
    ppermute x3, starting transfers between devices, shards(): lax.ppermute(counts, 'ta', [(i, i ^ by) for i in range(ta_count)])  3.27 us
    pallas_call x1, Pallas kernels, shards(): pl.pallas_call(adjoint_kernel, in_specs=[VMEM, VMEM, VMEM], out_specs=VME...  1.74 us
    ppermute x3, waiting for transfers between devices, shards(): lax.ppermute(counts, 'ta', [(i, i ^ by) for i in range(ta_count)])  1.41 us
  transfers between devices with their start and end apart: 5, of which 1 were waited for; matrix products, arithmetic and copies ran while one was open for 0% of the time, Pallas kernels for 9%

profile of v3, /device:TPU:1, one launch (start us, length us, event | category | flops | bytes accessed | tf_op | source)
XLA Modules:
  0.0 56.9 jit_solution(17851337251879582426)
XLA Ops:
  0.6 4.6 %collective-permute-start.1 = (f32[128,128]{1,0:T(8,128)}, f32[128,128]{1,0:T(8,128)S(1)}, u32[]{:S(2)}, u32[]{:S(2)}) collective-permute-start(f32[128,128]{1,0:T(8,128)} %bitcast.23), channel_id=1, source_target_pairs={{4,8},{8,4},{12,16},{16,12},{20,24},{24,20},{28,32},{32,28},{36,40... | collective-permute-start | bytes 196616 | tf_op jit(solution)/shard_map/ppermute | solution.py:433
  5.2 0.1 collective-permute-start
  5.3 3.6 %legendre.1 = (f32[128,24,128]{2,1,0:T(8,128)S(1)}, f32[128,128]{1,0:T(8,128)S(1)}, s32[8,128]{1,0:T(8,128)S(1)}, f32[2,128,128]{2,1,0:T(8,128)S(1)}, bf16[128,2...) custom-call(s32[64]{0:T(128)} %orders_in.1, ...), custom_call_target="tpu_custom_call" | custom-call | tf_op jit(solution)/shard_map/legendre/pallas_call | solution.py:438
  9.0 0.0 collective-permute-done.1.across
  9.0 0.0 collective-permute-done.within
  9.0 21.8 %all_to_all.22 = f32[64,2,128]{2,1,0:T(2,128)S(1)} all-to-all(f32[64,2,128]{2,1,0:T(2,128)S(1)} %bitcast.19), channel_id=1, replica_groups=mesh['ma'=64,'ta'=4] {'ma'}, dimensions={0} | all-to-all | bytes 131072 | tf_op jit(solution)/shard_map/all_to_all | solution.py:473
  30.8 5.2 %euler.1 = (f32[2,128,128]{2,1,0:T(8,128)}, f32[128,128]{1,0:T(8,128)S(1)}) custom-call(f32[2,32]{1,0:T(2,128)S(1)} %get-tuple-element.17.level_weights, f32[2,128,128]{2,1,0:T(8,128)S(1)} %get-tuple-element.18.turns, bf16[128,256]{1,0:T(8,128)(2,1)S(1)} %get-tuple-element.19.basis, bf16[128,256]{1,0:T(8,128)(2,1)S(1)} %get-tuple-element.20.basis_turned, ...), custom_call_target="tpu_custom_call" | custom-call | tf_op jit(solution)/shard_map/euler/pallas_call | solution.py:474
  36.1 13.6 %all_to_all.23 = f32[64,2,128]{2,1,0:T(2,128)S(1)} all-to-all(f32[64,2,128]{2,1,0:T(2,128)S(1)} %bitcast.20), channel_id=1, replica_groups=mesh['ma'=64,'ta'=4] {'ma'}, dimensions={0} | all-to-all | bytes 131072 | tf_op jit(solution)/shard_map/all_to_all | solution.py:500
  49.7 0.1 slice_reduce_fusion
  49.8 0.1 reshape.41
  49.9 2.5 %collective-permute-start.4 = (f32[2,32]{1,0:T(2,128)S(1)}, f32[2,32]{1,0:T(2,128)S(1)}, u32[]{:S(2)}, u32[]{:S(2)}) collective-permute-start(f32[2,32]{1,0:T(2,128)S(1)} %reshape.41), channel_id=1, source_target_pairs={{0,3},{1,2},{2,1},{3,0},{4,7},{5,6},{6,5},{7,4},{8,11},{9,10},{10,... | collective-permute-start | bytes 776 | tf_op jit(solution)/shard_map/ppermute | solution.py:502
  52.4 0.5 collective-permute-start.3
  52.9 0.3 collective-permute-start.2
  53.2 1.7 %adjoint.1 = f32[2,128,128]{2,1,0:T(8,128)} custom-call(s32[8,128]{1,0:T(8,128)S(1)} %get-tuple-element.29.order_rows, f32[128,128]{1,0:T(8,128)S(1)} %bitcast.17, f32[128,24,128]{2,1,0:T(8,128)S(1)} %get-tuple-element.30.table), custom_call_target="tpu_custom_call" | custom-call | tf_op jit(solution)/shard_map/adjoint/pallas_call | solution.py:504
  54.9 0.0 collective-permute-done.4
  54.9 1.4 %collective-permute-done.3 = f32[2,32]{1,0:T(2,128)S(1)} collective-permute-done((f32[2,32]{1,0:T(2,128)S(1)}, f32[2,32]{1,0:T(2,128)S(1)}, u32[]{:S(2)}, u32[]{:S(2)}) %collective-permute-start.3) | collective-permute-done | bytes 288 | tf_op jit(solution)/shard_map/ppermute | solution.py:502
  56.3 0.0 collective-permute-done.2
  56.3 0.6 %add_multiply_fusion = f32[2,32]{1,0:T(2,128)} fusion(f32[2,32]{1,0:T(2,128)S(1)} %collective-permute-done.3, f32[2,32]{1,0:T(2,128)S(1)} %collective-permute-done.4, f32[2,32]{1,0:T(2,128)S(1)} %reshape.41, f32[2,32]{1,0:T(2,128)S(1)} %collective-permute-done.2), kind=kLoop, calls=%fused_computation.1 | loop fusion | flops 256 | bytes 1280 | tf_op jit(solution)/shard_map/div | solution.py:503
Async XLA Ops:
  0.6 8.4 %collective-permute-start.1 = (f32[128,128]{1,0:T(8,128)}, f32[128,128]{1,0:T(8,128)S(1)}, u32[]{:S(2)}, u32[]{:S(2)}) collective-permute-start(f32[128,128]{1,0:T(8,128)} %bitcast.23), channel_id=1, source_target_pairs={{4,8},{8,4},{12,16},{16,12},{20,24},{24,20},{28,32},{32,28},{36,40... | collective-permute-start | bytes 196616 | tf_op jit(solution)/shard_map/ppermute | solution.py:433
  5.2 3.8 %collective-permute-start = (f32[128,128]{1,0:T(8,128)}, f32[128,128]{1,0:T(8,128)S(1)}, u32[]{:S(2)}, u32[]{:S(2)}) collective-permute-start(f32[128,128]{1,0:T(8,128)} %bitcast.24), channel_id=1, source_target_pairs={{0,4},{4,0},{8,12},{12,8},{16,20},{20,16},{24,28},{28,24},{32,36},... | collective-permute-start | bytes 196616 | tf_op jit(solution)/shard_map/ppermute | solution.py:432
  49.9 5.0 %collective-permute-start.4 = (f32[2,32]{1,0:T(2,128)S(1)}, f32[2,32]{1,0:T(2,128)S(1)}, u32[]{:S(2)}, u32[]{:S(2)}) collective-permute-start(f32[2,32]{1,0:T(2,128)S(1)} %reshape.41), channel_id=1, source_target_pairs={{0,3},{1,2},{2,1},{3,0},{4,7},{5,6},{6,5},{7,4},{8,11},{9,10},{10,... | collective-permute-start | bytes 776 | tf_op jit(solution)/shard_map/ppermute | solution.py:502
  52.4 3.9 %collective-permute-start.3 = (f32[2,32]{1,0:T(2,128)S(1)}, f32[2,32]{1,0:T(2,128)S(1)}, u32[]{:S(2)}, u32[]{:S(2)}) collective-permute-start(f32[2,32]{1,0:T(2,128)S(1)} %reshape.41), channel_id=1, source_target_pairs={{0,2},{1,3},{2,0},{3,1},{4,6},{5,7},{6,4},{7,5},{8,10},{9,11},{10,... | collective-permute-start | bytes 776 | tf_op jit(solution)/shard_map/ppermute | solution.py:502
  52.9 3.4 %collective-permute-start.2 = (f32[2,32]{1,0:T(2,128)S(1)}, f32[2,32]{1,0:T(2,128)S(1)}, u32[]{:S(2)}, u32[]{:S(2)}) collective-permute-start(f32[2,32]{1,0:T(2,128)S(1)} %reshape.41), channel_id=1, source_target_pairs={{0,1},{1,0},{2,3},{3,2},{4,5},{5,4},{6,7},{7,6},{8,9},{9,8},{10,11... | collective-permute-start | bytes 776 | tf_op jit(solution)/shard_map/ppermute | solution.py:502

commit v4 on v3

--- a/solution.py
+++ b/solution.py
@@ -430,7 +430,7 @@
     ma_count = lax.axis_size("ma")
     noise = noise_weight.reshape(SIDE, SIDE)
     within = lax.ppermute(noise, "ma", [(i, i ^ 1) for i in range(ma_count)])
-    across = lax.ppermute(noise, "ma", [(i, i + 1 if i % 2 else i - 1) for i in range(1, ma_count - 1)])
+    across = lax.ppermute(noise, "ma", [(i, (i + (1 if i % 2 else -1)) % ma_count) for i in range(ma_count)])
     packed = harmonics.reshape(2, 2, 64, SIDE).transpose(0, 2, 1, 3).reshape(2, SIDE, SIDE)
     square = jax.ShapeDtypeStruct((2 * CYCLES, SIDE), F32)
     orders_there = pltpu.with_memory_space_constraint(order_table, pltpu.HBM)

time: 57.1 us -> 55.2 us (0.967)
  blocking collectives: 35.4 us -> 28.9 us
  starting transfers between devices: 7.95 us -> 12.6 us
    all_to_all x2, blocking collectives: 35.4 us -> 28.9 us  [shards(): lax.all_to_all(sent, 'ma', split_axis=0, concat_axis=0, tiled=True)]
    ppermute x1, starting transfers between devices: 0.09 us -> 6.56 us  [shards(): within = lax.ppermute(noise, 'ma', [(i, i ^ 1) for i in range(ma_count)])]
    ppermute x1, starting transfers between devices: 4.59 us -> 2.77 us  [shards(): lax.ppermute(noise, 'ma', [(i, (i + (1 if i % 2 else -1)) % ma_count) for...]
  transfers between devices with their start and end apart: 5 -> 5, of which waited for: 1 -> 1; matrix products, arithmetic and copies ran while one was open for 0% -> 0% of each run, Pallas kernels for 9% -> 10%
where the time goes in v4:
time: 55.2 us; the launch traced here: 55.1 us
  blocking collectives  28.9 us (52%)
  starting transfers between devices  12.6 us (23%)
  Pallas kernels  10.6 us (19%)
  waiting for transfers between devices  1.46 us (3%)
  other arithmetic  0.72 us (1%)
  between operations  0.67 us (1%)
    all_to_all x2, blocking collectives, shards(): lax.all_to_all(sent, 'ma', split_axis=0, concat_axis=0, tiled=True)  28.9 us
    ppermute x1, starting transfers between devices, shards(): within = lax.ppermute(noise, 'ma', [(i, i ^ 1) for i in range(ma_count)])  6.56 us
    pallas_call x1, Pallas kernels, shards(): pl.pallas_call(euler_kernel, in_specs=[SMEM] + [VMEM] * 8, out_specs=[HBM...  5.25 us
    pallas_call x1, Pallas kernels, shards(): pl.pallas_call(legendre_kernel, in_specs=[HBM] * 5, out_specs=[VMEM] * 9,...  3.65 us
    ppermute x3, starting transfers between devices, shards(): lax.ppermute(counts, 'ta', [(i, i ^ by) for i in range(ta_count)])  3.27 us
    ppermute x1, starting transfers between devices, shards(): lax.ppermute(noise, 'ma', [(i, (i + (1 if i % 2 else -1)) % ma_count) for...  2.77 us
    pallas_call x1, Pallas kernels, shards(): pl.pallas_call(adjoint_kernel, in_specs=[VMEM, VMEM, VMEM], out_specs=VME...  1.74 us
    ppermute x3, waiting for transfers between devices, shards(): lax.ppermute(counts, 'ta', [(i, i ^ by) for i in range(ta_count)])  1.45 us
  transfers between devices with their start and end apart: 5, of which 1 were waited for; matrix products, arithmetic and copies ran while one was open for 0% of the time, Pallas kernels for 10%

profile of v4, /device:TPU:1, one launch (start us, length us, event | category | flops | bytes accessed | tf_op | source)
XLA Modules:
  0.0 55.1 jit_solution(16273145376891798735)
XLA Ops:
  0.6 2.8 %collective-permute-start.1 = (f32[128,128]{1,0:T(8,128)}, f32[128,128]{1,0:T(8,128)S(1)}, u32[]{:S(2)}, u32[]{:S(2)}) collective-permute-start(f32[128,128]{1,0:T(8,128)} %bitcast.23), channel_id=1, source_target_pairs={{0,252},{4,8},{8,4},{12,16},{16,12},{20,24},{24,20},{28,32},{32,28... | collective-permute-start | bytes 196616 | tf_op jit(solution)/shard_map/ppermute | solution.py:433
  3.4 6.6 %collective-permute-start = (f32[128,128]{1,0:T(8,128)}, f32[128,128]{1,0:T(8,128)S(1)}, u32[]{:S(2)}, u32[]{:S(2)}) collective-permute-start(f32[128,128]{1,0:T(8,128)} %bitcast.24), channel_id=1, source_target_pairs={{0,4},{4,0},{8,12},{12,8},{16,20},{20,16},{24,28},{28,24},{32,36},... | collective-permute-start | bytes 196616 | tf_op jit(solution)/shard_map/ppermute | solution.py:432
  10.0 3.6 %legendre.1 = (f32[128,24,128]{2,1,0:T(8,128)S(1)}, f32[128,128]{1,0:T(8,128)S(1)}, s32[8,128]{1,0:T(8,128)S(1)}, f32[2,128,128]{2,1,0:T(8,128)S(1)}, bf16[128,2...) custom-call(s32[64]{0:T(128)} %orders_in.1, ...), custom_call_target="tpu_custom_call" | custom-call | tf_op jit(solution)/shard_map/legendre/pallas_call | solution.py:438
  13.6 0.0 collective-permute-done.1.across
  13.6 0.0 collective-permute-done.within
  13.6 15.4 %all_to_all.22 = f32[64,2,128]{2,1,0:T(2,128)S(1)} all-to-all(f32[64,2,128]{2,1,0:T(2,128)S(1)} %bitcast.19), channel_id=1, replica_groups=mesh['ma'=64,'ta'=4] {'ma'}, dimensions={0} | all-to-all | bytes 131072 | tf_op jit(solution)/shard_map/all_to_all | solution.py:473
  29.0 5.3 %euler.1 = (f32[2,128,128]{2,1,0:T(8,128)}, f32[128,128]{1,0:T(8,128)S(1)}) custom-call(f32[2,32]{1,0:T(2,128)S(1)} %get-tuple-element.17.level_weights, f32[2,128,128]{2,1,0:T(8,128)S(1)} %get-tuple-element.18.turns, bf16[128,256]{1,0:T(8,128)(2,1)S(1)} %get-tuple-element.19.basis, bf16[128,256]{1,0:T(8,128)(2,1)S(1)} %get-tuple-element.20.basis_turned, ...), custom_call_target="tpu_custom_call" | custom-call | tf_op jit(solution)/shard_map/euler/pallas_call | solution.py:474
  34.3 13.5 %all_to_all.23 = f32[64,2,128]{2,1,0:T(2,128)S(1)} all-to-all(f32[64,2,128]{2,1,0:T(2,128)S(1)} %bitcast.20), channel_id=1, replica_groups=mesh['ma'=64,'ta'=4] {'ma'}, dimensions={0} | all-to-all | bytes 131072 | tf_op jit(solution)/shard_map/all_to_all | solution.py:500
  47.8 0.1 slice_reduce_fusion
  48.0 0.1 reshape.41
  48.0 2.5 %collective-permute-start.4 = (f32[2,32]{1,0:T(2,128)S(1)}, f32[2,32]{1,0:T(2,128)S(1)}, u32[]{:S(2)}, u32[]{:S(2)}) collective-permute-start(f32[2,32]{1,0:T(2,128)S(1)} %reshape.41), channel_id=1, source_target_pairs={{0,3},{1,2},{2,1},{3,0},{4,7},{5,6},{6,5},{7,4},{8,11},{9,10},{10,... | collective-permute-start | bytes 776 | tf_op jit(solution)/shard_map/ppermute | solution.py:502
  50.6 0.5 collective-permute-start.3
  51.1 0.2 collective-permute-start.2
  51.3 1.7 %adjoint.1 = f32[2,128,128]{2,1,0:T(8,128)} custom-call(s32[8,128]{1,0:T(8,128)S(1)} %get-tuple-element.29.order_rows, f32[128,128]{1,0:T(8,128)S(1)} %bitcast.17, f32[128,24,128]{2,1,0:T(8,128)S(1)} %get-tuple-element.30.table), custom_call_target="tpu_custom_call" | custom-call | tf_op jit(solution)/shard_map/adjoint/pallas_call | solution.py:504
  53.1 0.0 collective-permute-done.4
  53.1 1.4 %collective-permute-done.3 = f32[2,32]{1,0:T(2,128)S(1)} collective-permute-done((f32[2,32]{1,0:T(2,128)S(1)}, f32[2,32]{1,0:T(2,128)S(1)}, u32[]{:S(2)}, u32[]{:S(2)}) %collective-permute-start.3) | collective-permute-done | bytes 288 | tf_op jit(solution)/shard_map/ppermute | solution.py:502
  54.5 0.0 collective-permute-done.2
  54.5 0.6 %add_multiply_fusion = f32[2,32]{1,0:T(2,128)} fusion(f32[2,32]{1,0:T(2,128)S(1)} %collective-permute-done.3, f32[2,32]{1,0:T(2,128)S(1)} %collective-permute-done.4, f32[2,32]{1,0:T(2,128)S(1)} %reshape.41, f32[2,32]{1,0:T(2,128)S(1)} %collective-permute-done.2), kind=kLoop, calls=%fused_computation.1 | loop fusion | flops 256 | bytes 1280 | tf_op jit(solution)/shard_map/div | solution.py:503
Async XLA Ops:
  0.6 13.0 %collective-permute-start.1 = (f32[128,128]{1,0:T(8,128)}, f32[128,128]{1,0:T(8,128)S(1)}, u32[]{:S(2)}, u32[]{:S(2)}) collective-permute-start(f32[128,128]{1,0:T(8,128)} %bitcast.23), channel_id=1, source_target_pairs={{0,252},{4,8},{8,4},{12,16},{16,12},{20,24},{24,20},{28,32},{32,28... | collective-permute-start | bytes 196616 | tf_op jit(solution)/shard_map/ppermute | solution.py:433
  3.4 10.2 %collective-permute-start = (f32[128,128]{1,0:T(8,128)}, f32[128,128]{1,0:T(8,128)S(1)}, u32[]{:S(2)}, u32[]{:S(2)}) collective-permute-start(f32[128,128]{1,0:T(8,128)} %bitcast.24), channel_id=1, source_target_pairs={{0,4},{4,0},{8,12},{12,8},{16,20},{20,16},{24,28},{28,24},{32,36},... | collective-permute-start | bytes 196616 | tf_op jit(solution)/shard_map/ppermute | solution.py:432
  48.0 5.0 %collective-permute-start.4 = (f32[2,32]{1,0:T(2,128)S(1)}, f32[2,32]{1,0:T(2,128)S(1)}, u32[]{:S(2)}, u32[]{:S(2)}) collective-permute-start(f32[2,32]{1,0:T(2,128)S(1)} %reshape.41), channel_id=1, source_target_pairs={{0,3},{1,2},{2,1},{3,0},{4,7},{5,6},{6,5},{7,4},{8,11},{9,10},{10,... | collective-permute-start | bytes 776 | tf_op jit(solution)/shard_map/ppermute | solution.py:502
  50.6 3.9 %collective-permute-start.3 = (f32[2,32]{1,0:T(2,128)S(1)}, f32[2,32]{1,0:T(2,128)S(1)}, u32[]{:S(2)}, u32[]{:S(2)}) collective-permute-start(f32[2,32]{1,0:T(2,128)S(1)} %reshape.41), channel_id=1, source_target_pairs={{0,2},{1,3},{2,0},{3,1},{4,6},{5,7},{6,4},{7,5},{8,10},{9,11},{10,... | collective-permute-start | bytes 776 | tf_op jit(solution)/shard_map/ppermute | solution.py:502
  51.1 3.4 %collective-permute-start.2 = (f32[2,32]{1,0:T(2,128)S(1)}, f32[2,32]{1,0:T(2,128)S(1)}, u32[]{:S(2)}, u32[]{:S(2)}) collective-permute-start(f32[2,32]{1,0:T(2,128)S(1)} %reshape.41), channel_id=1, source_target_pairs={{0,1},{1,0},{2,3},{3,2},{4,5},{5,4},{6,7},{7,6},{8,9},{9,8},{10,11... | collective-permute-start | bytes 776 | tf_op jit(solution)/shard_map/ppermute | solution.py:502

commit v5 on v4

--- a/solution.py
+++ b/solution.py
@@ -249,13 +249,6 @@
             lefts.append(jnp.where(real_row, real, -imag) * a_cos - jnp.where(real_row, imag, real) * a_sin)
     maps = both_halves(basis_turned[...], jnp.concatenate(lefts, axis=1))
 
-    for r in range(2):
-        for v in range(16):
-            flips[r, pl.ds(v, 8, stride=16), :] = maps[8 * v : 8 * v + 8, r * SIDE : (r + 1) * SIDE]
-        kappa[r] = flips[r].T
-    keep_kappa = pltpu.make_async_copy(kappa, kappa_out, sems.at[0])
-    keep_kappa.start()
-
     def arranged(x, slot):
         flips[slot] = x.T
         return jnp.concatenate([flips[slot, pl.ds(v, 8, stride=16), :] for v in range(16)], axis=0)
@@ -280,6 +273,13 @@
             fields[r, n, :8, :] = jnp.where(sub == 0, pltpu.roll(last, 1, 1), last)
             first = pltpu.roll(x[:8], 7, 0)
             fields[r, n, 8 + SIDE :, :] = jnp.where(sub == 7, pltpu.roll(first, SIDE - 1, 1), first)
+    for r in range(2):
+        for v in range(16):
+            flips[r, pl.ds(v, 8, stride=16), :] = maps[8 * v : 8 * v + 8, r * SIDE : (r + 1) * SIDE]
+        kappa[r] = flips[r].T
+    keep_kappa = pltpu.make_async_copy(kappa, kappa_out, sems.at[0])
+    keep_kappa.start()
+
     gradients[...] = jnp.zeros_like(gradients)
 
     def levels(r, group, odd, top):

time: 55.2 us -> 55.2 us (level)
  no operation moved by 1% of the time
where the time goes in v5:
time: 55.2 us; the launch traced here: 55 us
  blocking collectives  29 us (53%)
  starting transfers between devices  12.6 us (23%)
  Pallas kernels  10.6 us (19%)
  waiting for transfers between devices  1.41 us (3%)
  other arithmetic  0.72 us (1%)
  between operations  0.67 us (1%)
    all_to_all x2, blocking collectives, shards(): lax.all_to_all(sent, 'ma', split_axis=0, concat_axis=0, tiled=True)  29 us
    ppermute x1, starting transfers between devices, shards(): within = lax.ppermute(noise, 'ma', [(i, i ^ 1) for i in range(ma_count)])  6.56 us
    pallas_call x1, Pallas kernels, shards(): pl.pallas_call(euler_kernel, in_specs=[SMEM] + [VMEM] * 8, out_specs=[HBM...  5.19 us
    pallas_call x1, Pallas kernels, shards(): pl.pallas_call(legendre_kernel, in_specs=[HBM] * 5, out_specs=[VMEM] * 9,...  3.65 us
    ppermute x3, starting transfers between devices, shards(): lax.ppermute(counts, 'ta', [(i, i ^ by) for i in range(ta_count)])  3.27 us
    ppermute x1, starting transfers between devices, shards(): lax.ppermute(noise, 'ma', [(i, (i + (1 if i % 2 else -1)) % ma_count) for...  2.77 us
    pallas_call x1, Pallas kernels, shards(): pl.pallas_call(adjoint_kernel, in_specs=[VMEM, VMEM, VMEM], out_specs=VME...  1.74 us
    ppermute x3, waiting for transfers between devices, shards(): lax.ppermute(counts, 'ta', [(i, i ^ by) for i in range(ta_count)])  1.41 us
  transfers between devices with their start and end apart: 5, of which 1 were waited for; matrix products, arithmetic and copies ran while one was open for 0% of the time, Pallas kernels for 10%

profile of v5, /device:TPU:1, one launch (start us, length us, event | category | flops | bytes accessed | tf_op | source)
XLA Modules:
  0.0 55.0 jit_solution(553095799111717982)
XLA Ops:
  0.6 2.8 %collective-permute-start.1 = (f32[128,128]{1,0:T(8,128)}, f32[128,128]{1,0:T(8,128)S(1)}, u32[]{:S(2)}, u32[]{:S(2)}) collective-permute-start(f32[128,128]{1,0:T(8,128)} %bitcast.23), channel_id=1, source_target_pairs={{0,252},{4,8},{8,4},{12,16},{16,12},{20,24},{24,20},{28,32},{32,28... | collective-permute-start | bytes 196616 | tf_op jit(solution)/shard_map/ppermute | solution.py:433
  3.4 6.6 %collective-permute-start = (f32[128,128]{1,0:T(8,128)}, f32[128,128]{1,0:T(8,128)S(1)}, u32[]{:S(2)}, u32[]{:S(2)}) collective-permute-start(f32[128,128]{1,0:T(8,128)} %bitcast.24), channel_id=1, source_target_pairs={{0,4},{4,0},{8,12},{12,8},{16,20},{20,16},{24,28},{28,24},{32,36},... | collective-permute-start | bytes 196616 | tf_op jit(solution)/shard_map/ppermute | solution.py:432
  10.0 3.6 %legendre.1 = (f32[128,24,128]{2,1,0:T(8,128)S(1)}, f32[128,128]{1,0:T(8,128)S(1)}, s32[8,128]{1,0:T(8,128)S(1)}, f32[2,128,128]{2,1,0:T(8,128)S(1)}, bf16[128,2...) custom-call(s32[64]{0:T(128)} %orders_in.1, ...), custom_call_target="tpu_custom_call" | custom-call | tf_op jit(solution)/shard_map/legendre/pallas_call | solution.py:438
  13.6 0.0 collective-permute-done.1.across
  13.6 0.0 collective-permute-done.within
  13.6 15.4 %all_to_all.22 = f32[64,2,128]{2,1,0:T(2,128)S(1)} all-to-all(f32[64,2,128]{2,1,0:T(2,128)S(1)} %bitcast.19), channel_id=1, replica_groups=mesh['ma'=64,'ta'=4] {'ma'}, dimensions={0} | all-to-all | bytes 131072 | tf_op jit(solution)/shard_map/all_to_all | solution.py:473
  29.0 5.2 %euler.1 = (f32[2,128,128]{2,1,0:T(8,128)}, f32[128,128]{1,0:T(8,128)S(1)}) custom-call(f32[2,32]{1,0:T(2,128)S(1)} %get-tuple-element.17.level_weights, f32[2,128,128]{2,1,0:T(8,128)S(1)} %get-tuple-element.18.turns, bf16[128,256]{1,0:T(8,128)(2,1)S(1)} %get-tuple-element.19.basis, bf16[128,256]{1,0:T(8,128)(2,1)S(1)} %get-tuple-element.20.basis_turned, ...), custom_call_target="tpu_custom_call" | custom-call | tf_op jit(solution)/shard_map/euler/pallas_call | solution.py:474
  34.2 13.6 %all_to_all.23 = f32[64,2,128]{2,1,0:T(2,128)S(1)} all-to-all(f32[64,2,128]{2,1,0:T(2,128)S(1)} %bitcast.20), channel_id=1, replica_groups=mesh['ma'=64,'ta'=4] {'ma'}, dimensions={0} | all-to-all | bytes 131072 | tf_op jit(solution)/shard_map/all_to_all | solution.py:500
  47.8 0.1 slice_reduce_fusion
  48.0 0.1 reshape.41
  48.0 2.5 %collective-permute-start.4 = (f32[2,32]{1,0:T(2,128)S(1)}, f32[2,32]{1,0:T(2,128)S(1)}, u32[]{:S(2)}, u32[]{:S(2)}) collective-permute-start(f32[2,32]{1,0:T(2,128)S(1)} %reshape.41), channel_id=1, source_target_pairs={{0,3},{1,2},{2,1},{3,0},{4,7},{5,6},{6,5},{7,4},{8,11},{9,10},{10,... | collective-permute-start | bytes 776 | tf_op jit(solution)/shard_map/ppermute | solution.py:502
  50.5 0.5 collective-permute-start.3
  51.0 0.3 collective-permute-start.2
  51.3 1.7 %adjoint.1 = f32[2,128,128]{2,1,0:T(8,128)} custom-call(s32[8,128]{1,0:T(8,128)S(1)} %get-tuple-element.29.order_rows, f32[128,128]{1,0:T(8,128)S(1)} %bitcast.17, f32[128,24,128]{2,1,0:T(8,128)S(1)} %get-tuple-element.30.table), custom_call_target="tpu_custom_call" | custom-call | tf_op jit(solution)/shard_map/adjoint/pallas_call | solution.py:504
  53.0 0.0 collective-permute-done.4
  53.0 1.4 %collective-permute-done.3 = f32[2,32]{1,0:T(2,128)S(1)} collective-permute-done((f32[2,32]{1,0:T(2,128)S(1)}, f32[2,32]{1,0:T(2,128)S(1)}, u32[]{:S(2)}, u32[]{:S(2)}) %collective-permute-start.3) | collective-permute-done | bytes 288 | tf_op jit(solution)/shard_map/ppermute | solution.py:502
  54.5 0.0 collective-permute-done.2
  54.5 0.6 %add_multiply_fusion = f32[2,32]{1,0:T(2,128)} fusion(f32[2,32]{1,0:T(2,128)S(1)} %collective-permute-done.3, f32[2,32]{1,0:T(2,128)S(1)} %collective-permute-done.4, f32[2,32]{1,0:T(2,128)S(1)} %reshape.41, f32[2,32]{1,0:T(2,128)S(1)} %collective-permute-done.2), kind=kLoop, calls=%fused_computation.1 | loop fusion | flops 256 | bytes 1280 | tf_op jit(solution)/shard_map/div | solution.py:503
Async XLA Ops:
  0.6 13.0 %collective-permute-start.1 = (f32[128,128]{1,0:T(8,128)}, f32[128,128]{1,0:T(8,128)S(1)}, u32[]{:S(2)}, u32[]{:S(2)}) collective-permute-start(f32[128,128]{1,0:T(8,128)} %bitcast.23), channel_id=1, source_target_pairs={{0,252},{4,8},{8,4},{12,16},{16,12},{20,24},{24,20},{28,32},{32,28... | collective-permute-start | bytes 196616 | tf_op jit(solution)/shard_map/ppermute | solution.py:433
  3.4 10.2 %collective-permute-start = (f32[128,128]{1,0:T(8,128)}, f32[128,128]{1,0:T(8,128)S(1)}, u32[]{:S(2)}, u32[]{:S(2)}) collective-permute-start(f32[128,128]{1,0:T(8,128)} %bitcast.24), channel_id=1, source_target_pairs={{0,4},{4,0},{8,12},{12,8},{16,20},{20,16},{24,28},{28,24},{32,36},... | collective-permute-start | bytes 196616 | tf_op jit(solution)/shard_map/ppermute | solution.py:432
  48.0 5.0 %collective-permute-start.4 = (f32[2,32]{1,0:T(2,128)S(1)}, f32[2,32]{1,0:T(2,128)S(1)}, u32[]{:S(2)}, u32[]{:S(2)}) collective-permute-start(f32[2,32]{1,0:T(2,128)S(1)} %reshape.41), channel_id=1, source_target_pairs={{0,3},{1,2},{2,1},{3,0},{4,7},{5,6},{6,5},{7,4},{8,11},{9,10},{10,... | collective-permute-start | bytes 776 | tf_op jit(solution)/shard_map/ppermute | solution.py:502
  50.5 3.9 %collective-permute-start.3 = (f32[2,32]{1,0:T(2,128)S(1)}, f32[2,32]{1,0:T(2,128)S(1)}, u32[]{:S(2)}, u32[]{:S(2)}) collective-permute-start(f32[2,32]{1,0:T(2,128)S(1)} %reshape.41), channel_id=1, source_target_pairs={{0,2},{1,3},{2,0},{3,1},{4,6},{5,7},{6,4},{7,5},{8,10},{9,11},{10,... | collective-permute-start | bytes 776 | tf_op jit(solution)/shard_map/ppermute | solution.py:502
  51.0 3.4 %collective-permute-start.2 = (f32[2,32]{1,0:T(2,128)S(1)}, f32[2,32]{1,0:T(2,128)S(1)}, u32[]{:S(2)}, u32[]{:S(2)}) collective-permute-start(f32[2,32]{1,0:T(2,128)S(1)} %reshape.41), channel_id=1, source_target_pairs={{0,1},{1,0},{2,3},{3,2},{4,5},{5,4},{6,7},{7,6},{8,9},{9,8},{10,11... | collective-permute-start | bytes 776 | tf_op jit(solution)/shard_map/ppermute | solution.py:502

commit v6 on v5

--- a/solution.py
+++ b/solution.py
@@ -314,11 +314,12 @@
 
     def sweep(odd, top):
         def step(group, carry):
-            for r in range(2):
-                levels(r, group, odd, top)
+            for more in range(2):
+                for r in range(2):
+                    levels(r, 2 * group + more, odd, top)
             return carry
 
-        lax.fori_loop(0, LEVELS // GROUP, step, 0)
+        lax.fori_loop(0, LEVELS // GROUP // 2, step, 0)
 
     pl.when(cycle == 0)(lambda: sweep(True, True))
     pl.when((cycle > 0) & (parity == 1))(lambda: sweep(True, False))

time: 55.2 us -> 55.1 us (level)
  no operation moved by 1% of the time
where the time goes in v6:
time: 55.1 us; the launch traced here: 54.9 us
  blocking collectives  28.8 us (52%)
  starting transfers between devices  12.6 us (23%)
  Pallas kernels  10.6 us (19%)
  waiting for transfers between devices  1.41 us (3%)
  other arithmetic  0.72 us (1%)
  between operations  0.67 us (1%)
    all_to_all x2, blocking collectives, shards(): lax.all_to_all(sent, 'ma', split_axis=0, concat_axis=0, tiled=True)  28.8 us
    ppermute x1, starting transfers between devices, shards(): within = lax.ppermute(noise, 'ma', [(i, i ^ 1) for i in range(ma_count)])  6.56 us
    pallas_call x1, Pallas kernels, shards(): pl.pallas_call(euler_kernel, in_specs=[SMEM] + [VMEM] * 8, out_specs=[HBM...  5.19 us
    pallas_call x1, Pallas kernels, shards(): pl.pallas_call(legendre_kernel, in_specs=[HBM] * 5, out_specs=[VMEM] * 9,...  3.65 us
    ppermute x3, starting transfers between devices, shards(): lax.ppermute(counts, 'ta', [(i, i ^ by) for i in range(ta_count)])  3.27 us
    ppermute x1, starting transfers between devices, shards(): lax.ppermute(noise, 'ma', [(i, (i + (1 if i % 2 else -1)) % ma_count) for...  2.77 us
    pallas_call x1, Pallas kernels, shards(): pl.pallas_call(adjoint_kernel, in_specs=[VMEM, VMEM, VMEM], out_specs=VME...  1.74 us
    ppermute x3, waiting for transfers between devices, shards(): lax.ppermute(counts, 'ta', [(i, i ^ by) for i in range(ta_count)])  1.41 us
  transfers between devices with their start and end apart: 5, of which 1 were waited for; matrix products, arithmetic and copies ran while one was open for 0% of the time, Pallas kernels for 10%

profile of v6, /device:TPU:1, one launch (start us, length us, event | category | flops | bytes accessed | tf_op | source)
XLA Modules:
  0.0 54.9 jit_solution(1328631454881187965)
XLA Ops:
  0.6 2.8 %collective-permute-start.1 = (f32[128,128]{1,0:T(8,128)}, f32[128,128]{1,0:T(8,128)S(1)}, u32[]{:S(2)}, u32[]{:S(2)}) collective-permute-start(f32[128,128]{1,0:T(8,128)} %bitcast.23), channel_id=1, source_target_pairs={{0,252},{4,8},{8,4},{12,16},{16,12},{20,24},{24,20},{28,32},{32,28... | collective-permute-start | bytes 196616 | tf_op jit(solution)/shard_map/ppermute | solution.py:434
  3.4 6.6 %collective-permute-start = (f32[128,128]{1,0:T(8,128)}, f32[128,128]{1,0:T(8,128)S(1)}, u32[]{:S(2)}, u32[]{:S(2)}) collective-permute-start(f32[128,128]{1,0:T(8,128)} %bitcast.24), channel_id=1, source_target_pairs={{0,4},{4,0},{8,12},{12,8},{16,20},{20,16},{24,28},{28,24},{32,36},... | collective-permute-start | bytes 196616 | tf_op jit(solution)/shard_map/ppermute | solution.py:433
  10.0 3.6 %legendre.1 = (f32[128,24,128]{2,1,0:T(8,128)S(1)}, f32[128,128]{1,0:T(8,128)S(1)}, s32[8,128]{1,0:T(8,128)S(1)}, f32[2,128,128]{2,1,0:T(8,128)S(1)}, bf16[128,2...) custom-call(s32[64]{0:T(128)} %orders_in.1, ...), custom_call_target="tpu_custom_call" | custom-call | tf_op jit(solution)/shard_map/legendre/pallas_call | solution.py:439
  13.6 0.0 collective-permute-done.1.across
  13.6 0.0 collective-permute-done.within
  13.6 15.4 %all_to_all.22 = f32[64,2,128]{2,1,0:T(2,128)S(1)} all-to-all(f32[64,2,128]{2,1,0:T(2,128)S(1)} %bitcast.19), channel_id=1, replica_groups=mesh['ma'=64,'ta'=4] {'ma'}, dimensions={0} | all-to-all | bytes 131072 | tf_op jit(solution)/shard_map/all_to_all | solution.py:474
  29.0 5.2 %euler.1 = (f32[2,128,128]{2,1,0:T(8,128)}, f32[128,128]{1,0:T(8,128)S(1)}) custom-call(f32[2,32]{1,0:T(2,128)S(1)} %get-tuple-element.17.level_weights, f32[2,128,128]{2,1,0:T(8,128)S(1)} %get-tuple-element.18.turns, bf16[128,256]{1,0:T(8,128)(2,1)S(1)} %get-tuple-element.19.basis, bf16[128,256]{1,0:T(8,128)(2,1)S(1)} %get-tuple-element.20.basis_turned, ...), custom_call_target="tpu_custom_call" | custom-call | tf_op jit(solution)/shard_map/euler/pallas_call | solution.py:475
  34.2 13.5 %all_to_all.23 = f32[64,2,128]{2,1,0:T(2,128)S(1)} all-to-all(f32[64,2,128]{2,1,0:T(2,128)S(1)} %bitcast.20), channel_id=1, replica_groups=mesh['ma'=64,'ta'=4] {'ma'}, dimensions={0} | all-to-all | bytes 131072 | tf_op jit(solution)/shard_map/all_to_all | solution.py:501
  47.7 0.1 slice_reduce_fusion
  47.8 0.1 reshape.41
  47.9 2.5 %collective-permute-start.4 = (f32[2,32]{1,0:T(2,128)S(1)}, f32[2,32]{1,0:T(2,128)S(1)}, u32[]{:S(2)}, u32[]{:S(2)}) collective-permute-start(f32[2,32]{1,0:T(2,128)S(1)} %reshape.41), channel_id=1, source_target_pairs={{0,3},{1,2},{2,1},{3,0},{4,7},{5,6},{6,5},{7,4},{8,11},{9,10},{10,... | collective-permute-start | bytes 776 | tf_op jit(solution)/shard_map/ppermute | solution.py:503
  50.4 0.5 collective-permute-start.3
  50.9 0.3 collective-permute-start.2
  51.2 1.7 %adjoint.1 = f32[2,128,128]{2,1,0:T(8,128)} custom-call(s32[8,128]{1,0:T(8,128)S(1)} %get-tuple-element.29.order_rows, f32[128,128]{1,0:T(8,128)S(1)} %bitcast.17, f32[128,24,128]{2,1,0:T(8,128)S(1)} %get-tuple-element.30.table), custom_call_target="tpu_custom_call" | custom-call | tf_op jit(solution)/shard_map/adjoint/pallas_call | solution.py:505
  52.9 0.0 collective-permute-done.4
  52.9 1.4 %collective-permute-done.3 = f32[2,32]{1,0:T(2,128)S(1)} collective-permute-done((f32[2,32]{1,0:T(2,128)S(1)}, f32[2,32]{1,0:T(2,128)S(1)}, u32[]{:S(2)}, u32[]{:S(2)}) %collective-permute-start.3) | collective-permute-done | bytes 288 | tf_op jit(solution)/shard_map/ppermute | solution.py:503
  54.3 0.0 collective-permute-done.2
  54.3 0.6 %add_multiply_fusion = f32[2,32]{1,0:T(2,128)} fusion(f32[2,32]{1,0:T(2,128)S(1)} %collective-permute-done.3, f32[2,32]{1,0:T(2,128)S(1)} %collective-permute-done.4, f32[2,32]{1,0:T(2,128)S(1)} %reshape.41, f32[2,32]{1,0:T(2,128)S(1)} %collective-permute-done.2), kind=kLoop, calls=%fused_computation.1 | loop fusion | flops 256 | bytes 1280 | tf_op jit(solution)/shard_map/div | solution.py:504
Async XLA Ops:
  0.6 13.0 %collective-permute-start.1 = (f32[128,128]{1,0:T(8,128)}, f32[128,128]{1,0:T(8,128)S(1)}, u32[]{:S(2)}, u32[]{:S(2)}) collective-permute-start(f32[128,128]{1,0:T(8,128)} %bitcast.23), channel_id=1, source_target_pairs={{0,252},{4,8},{8,4},{12,16},{16,12},{20,24},{24,20},{28,32},{32,28... | collective-permute-start | bytes 196616 | tf_op jit(solution)/shard_map/ppermute | solution.py:434
  3.4 10.2 %collective-permute-start = (f32[128,128]{1,0:T(8,128)}, f32[128,128]{1,0:T(8,128)S(1)}, u32[]{:S(2)}, u32[]{:S(2)}) collective-permute-start(f32[128,128]{1,0:T(8,128)} %bitcast.24), channel_id=1, source_target_pairs={{0,4},{4,0},{8,12},{12,8},{16,20},{20,16},{24,28},{28,24},{32,36},... | collective-permute-start | bytes 196616 | tf_op jit(solution)/shard_map/ppermute | solution.py:433
  47.9 5.0 %collective-permute-start.4 = (f32[2,32]{1,0:T(2,128)S(1)}, f32[2,32]{1,0:T(2,128)S(1)}, u32[]{:S(2)}, u32[]{:S(2)}) collective-permute-start(f32[2,32]{1,0:T(2,128)S(1)} %reshape.41), channel_id=1, source_target_pairs={{0,3},{1,2},{2,1},{3,0},{4,7},{5,6},{6,5},{7,4},{8,11},{9,10},{10,... | collective-permute-start | bytes 776 | tf_op jit(solution)/shard_map/ppermute | solution.py:503
  50.4 3.9 %collective-permute-start.3 = (f32[2,32]{1,0:T(2,128)S(1)}, f32[2,32]{1,0:T(2,128)S(1)}, u32[]{:S(2)}, u32[]{:S(2)}) collective-permute-start(f32[2,32]{1,0:T(2,128)S(1)} %reshape.41), channel_id=1, source_target_pairs={{0,2},{1,3},{2,0},{3,1},{4,6},{5,7},{6,4},{7,5},{8,10},{9,11},{10,... | collective-permute-start | bytes 776 | tf_op jit(solution)/shard_map/ppermute | solution.py:503
  50.9 3.4 %collective-permute-start.2 = (f32[2,32]{1,0:T(2,128)S(1)}, f32[2,32]{1,0:T(2,128)S(1)}, u32[]{:S(2)}, u32[]{:S(2)}) collective-permute-start(f32[2,32]{1,0:T(2,128)S(1)} %reshape.41), channel_id=1, source_target_pairs={{0,1},{1,0},{2,3},{3,2},{4,5},{5,4},{6,7},{7,6},{8,9},{9,8},{10,11... | collective-permute-start | bytes 776 | tf_op jit(solution)/shard_map/ppermute | solution.py:503
